TPU v7x, 32 devices: a whole 2x2x4 slice. The times are simulated.
32 devices in a mesh: seq: 8 (over z, x), row: 4 (over y, core).
Axes of the slice: x: 2, y: 2, z: 4, core: 2. Of those that a mesh axis runs over, the one named last changes fastest.
Arguments:
- pixels: bfloat16 [16, 8192, 261], P('seq', 'row'), may hold values from -6 to 6
- pixel_seg: int32 [16, 8192], P('seq', 'row'), may hold values from -1 to 7, as said below
- latent_seg: int32 [16, 512], P('seq', 'row'), may hold values from 0 to 7
- latent_init: bfloat16 [512, 1024], P('row'), may hold values from -6 to 6
- cotangent: bfloat16 [16, 512, 1024], P('seq', 'row'), may hold values from -6 to 6
- pixel_gain: float32 [261], replicated, may hold values from 0.1 to 1.9
- query_gain: float32 [1024], replicated, may hold values from 0.1 to 1.9
- query_weight: bfloat16 [1024, 1024], replicated, may hold values from -0.1875 to 0.1875
- key_weight: bfloat16 [261, 1024], replicated, may hold values from -0.375 to 0.375
- value_weight: bfloat16 [261, 1024], replicated, may hold values from -0.375 to 0.375
- output_weight: bfloat16 [1024, 1024], replicated, may hold values from -6 to 6
- mlp_gain: float32 [1024], replicated, may hold values from 0.1 to 1.9
- up_weight: bfloat16 [1024, 1024], replicated, may hold values from -0.1875 to 0.1875
- down_weight: bfloat16 [1024, 1024], replicated, may hold values from -0.1875 to 0.1875
- self_gain: float32 [1024], replicated, may hold values from 0.1 to 1.9
- self_query: bfloat16 [1024, 1024], replicated, may hold values from -0.1875 to 0.1875
- self_key: bfloat16 [1024, 1024], replicated, may hold values from -0.1875 to 0.1875
- self_value: bfloat16 [1024, 1024], replicated, may hold values from -0.1875 to 0.1875
- self_output: bfloat16 [1024, 1024], replicated, may hold values from -1.5 to 1.5
- second_gain: float32 [1024], replicated, may hold values from 0.1 to 1.9
- second_up: bfloat16 [1024, 1024], replicated, may hold values from -0.1875 to 0.1875
- second_down: bfloat16 [1024, 1024], replicated, may hold values from -0.1875 to 0.1875
Outputs:
- latents: bfloat16 [16, 512, 1024], P('seq', 'row')
- pixel_grad: float32 [16, 8192, 261], P('seq', 'row')
- init_grad: float32 [512, 1024], P('row', 'seq')
- pixel_gain_grad: float32 [261], replicated
- query_gain_grad: float32 [1024], replicated
- mlp_gain_grad: float32 [1024], replicated
- self_gain_grad: float32 [1024], replicated
- second_gain_grad: float32 [1024], replicated
- query_weight_grad: float32 [1024, 1024], P(None, 'seq')
- key_weight_grad: float32 [261, 1024], P(None, 'seq')
- value_weight_grad: float32 [261, 1024], P(None, 'seq')
- output_weight_grad: float32 [1024, 1024], P(None, 'seq')
- up_weight_grad: float32 [1024, 1024], P(None, 'seq')
- down_weight_grad: float32 [1024, 1024], P(None, 'seq')
- self_query_grad: float32 [1024, 1024], P(None, 'seq')
- self_key_grad: float32 [1024, 1024], P(None, 'seq')
- self_value_grad: float32 [1024, 1024], P(None, 'seq')
- self_output_grad: float32 [1024, 1024], P(None, 'seq')
- second_up_grad: float32 [1024, 1024], P(None, 'seq')
- second_down_grad: float32 [1024, 1024], P(None, 'seq')
Inputs may be any that keep to these rules, and one draw needn't show every extreme that they name: `pixel_seg`: slot p of a sequence is empty (-1) or holds image p // 1024; each image fills the first half or more of its 1024 slots, and the last slot of each region is empty. `latent_seg`: every latent's image has pixels in its sequence.
All inputs are finite; a program needn't handle non-finite values.
Results may differ from a plain program's by a relative error of at most 0.023.
Values may be sent and summed in bfloat16 or wider, within the bound.
A program may use at most 512 MiB of HBM per device.

v0:
```python
import math

import jax
import jax.numpy as jnp
from jax import lax
from jax.sharding import PartitionSpec as P

HEADS = 8


EPSILON = 1e-05
NEGATIVE = -1000000000.0


def layer_norm(values, norm_gain):
    centre = values - jnp.mean(values, axis=-1, keepdims=True)
    spread = jnp.mean(centre * centre, axis=-1, keepdims=True)
    return centre * lax.rsqrt(spread + EPSILON) * norm_gain


def norm_back(values, norm_gain, upstream):
    unused, pullback = jax.vjp(layer_norm, values, norm_gain)
    return pullback(upstream)


def smooth(hidden):
    return jax.nn.gelu(hidden, approximate=False)


def smooth_back(hidden, upstream):
    unused, pullback = jax.vjp(smooth, hidden)
    return pullback(upstream)[0]


def matmul(former, latter):
    return jnp.dot(former, latter, preferred_element_type=jnp.float32)


def inner_left(former, latter):
    return lax.dot_general(
        former, latter, (((0,), (0,)), ((), ())), preferred_element_type=jnp.float32
    )


def inner_right(former, latter):
    return lax.dot_general(
        former, latter, (((1,), (1,)), ((), ())), preferred_element_type=jnp.float32
    )


def same_image(query_ids, key_ids):
    return query_ids.astype(jnp.float32)[:, None] == key_ids.astype(jnp.float32)[None, :]


def masked_scores(queries, keys, query_ids, key_ids, scale):
    scores = inner_right(queries, keys) * scale
    return jnp.where(same_image(query_ids, key_ids), scores, NEGATIVE)


def head_scores(queries, keys, query_ids, key_ids, scale):
    scores = jnp.einsum("qhd,khd->hqk", queries, keys, preferred_element_type=jnp.float32) * scale
    return jnp.where(same_image(query_ids, key_ids)[None], scores, NEGATIVE)


def mlp_forward(stream, norm_gain, up_matrix, down_matrix):
    normed = layer_norm(stream, norm_gain).astype(jnp.bfloat16)
    hidden = matmul(normed, up_matrix)
    active = smooth(hidden).astype(jnp.bfloat16)
    return (stream + matmul(active, down_matrix), (normed, hidden, active))


def mlp_backward(stream, norm_gain, up_matrix, down_matrix, stored, upstream):
    normed, hidden, active = stored
    branch = upstream.astype(jnp.bfloat16)
    down_part = inner_left(active, branch)
    active_grad = inner_right(branch, down_matrix).astype(jnp.bfloat16)
    hidden_grad = smooth_back(hidden, active_grad.astype(jnp.float32)).astype(jnp.bfloat16)
    up_part = inner_left(normed, hidden_grad)
    stream_grad, gain_part = norm_back(stream, norm_gain, inner_right(hidden_grad, up_matrix))
    return (upstream + stream_grad, gain_part, up_part, down_part)


def body(
    pixels,
    pixel_seg,
    latent_seg,
    latent_init,
    cotangent,
    pixel_gain,
    query_gain,
    query_weight,
    key_weight,
    value_weight,
    output_weight,
    mlp_gain,
    up_weight,
    down_weight,
    self_gain,
    self_query,
    self_key,
    self_value,
    self_output,
    second_gain,
    second_up,
    second_down,
):
    seq_count, pixel_rows, features = pixels.shape
    latent_rows, width = latent_init.shape
    head_count = HEADS
    head_width = width // head_count
    cross_scale = 1.0 / math.sqrt(width)
    self_scale = 1.0 / math.sqrt(head_width)
    init_float = latent_init.astype(jnp.float32)
    encoder_mats = (query_weight, key_weight, value_weight, output_weight, up_weight, down_weight)
    latent_mats = (self_query, self_key, self_value, self_output, second_up, second_down)
    early = [jnp.zeros(matrix.shape, jnp.float32) for matrix in encoder_mats]
    late = [jnp.zeros(matrix.shape, jnp.float32) for matrix in latent_mats]
    gain_sums = [
        jnp.zeros(vector.shape, jnp.float32)
        for vector in (pixel_gain, query_gain, mlp_gain, self_gain, second_gain)
    ]
    init_sum = jnp.zeros((latent_rows, width), jnp.float32)
    latent_list = []
    pixel_list = []
    for number in range(seq_count):
        pixel_float = pixels[number].astype(jnp.float32)
        pixel_ids = pixel_seg[number].astype(jnp.bfloat16)
        latent_ids = latent_seg[number].astype(jnp.bfloat16)
        pixel_normed = layer_norm(pixel_float, pixel_gain).astype(jnp.bfloat16)
        query_normed = layer_norm(init_float, query_gain).astype(jnp.bfloat16)
        queries = matmul(query_normed, query_weight).astype(jnp.bfloat16)
        own_keys = matmul(pixel_normed, key_weight).astype(jnp.bfloat16)
        own_values = matmul(pixel_normed, value_weight).astype(jnp.bfloat16)
        all_keys, all_values, key_ids = (
            lax.all_gather(own_keys, "row", axis=0, tiled=True),
            lax.all_gather(own_values, "row", axis=0, tiled=True),
            lax.all_gather(pixel_ids, "row", axis=0, tiled=True),
        )
        cross_scores = masked_scores(queries, all_keys, latent_ids, key_ids, cross_scale)
        cross_top = jnp.max(cross_scores, axis=1, keepdims=True)
        cross_exp = jnp.exp(cross_scores - cross_top)
        cross_total = jnp.sum(cross_exp, axis=1, keepdims=True)
        cross_lse = cross_top + jnp.log(cross_total)
        cross_probs = (cross_exp / cross_total).astype(jnp.bfloat16)
        attended = matmul(cross_probs, all_values).astype(jnp.bfloat16)
        stream_one = init_float + matmul(attended, output_weight)
        stream_two, first_kept = mlp_forward(stream_one, mlp_gain, up_weight, down_weight)
        self_normed = layer_norm(stream_two, self_gain).astype(jnp.bfloat16)
        self_queries = matmul(self_normed, self_query).astype(jnp.bfloat16)
        self_keys = matmul(self_normed, self_key).astype(jnp.bfloat16)
        self_values = matmul(self_normed, self_value).astype(jnp.bfloat16)
        key_all, value_all, id_all = (
            lax.all_gather(self_keys, "row", axis=0, tiled=True),
            lax.all_gather(self_values, "row", axis=0, tiled=True),
            lax.all_gather(latent_ids, "row", axis=0, tiled=True),
        )
        heads_query = self_queries.reshape(latent_rows, head_count, head_width)
        heads_key = key_all.reshape(-1, head_count, head_width)
        heads_value = value_all.reshape(-1, head_count, head_width)
        self_scores = head_scores(heads_query, heads_key, latent_ids, id_all, self_scale)
        self_top = jnp.max(self_scores, axis=2, keepdims=True)
        self_exp = jnp.exp(self_scores - self_top)
        self_total = jnp.sum(self_exp, axis=2, keepdims=True)
        self_lse = self_top + jnp.log(self_total)
        self_probs = (self_exp / self_total).astype(jnp.bfloat16)
        self_mixed = jnp.einsum(
            "hqk,khd->qhd", self_probs, heads_value, preferred_element_type=jnp.float32
        )
        self_mixed = self_mixed.reshape(latent_rows, width).astype(jnp.bfloat16)
        stream_three = stream_two + matmul(self_mixed, self_output)
        final_stream, second_kept = mlp_forward(stream_three, second_gain, second_up, second_down)
        latent_list.append(final_stream.astype(jnp.bfloat16))
        upstream = cotangent[number].astype(jnp.float32)
        upstream, gain_part, up_part, down_part = mlp_backward(
            stream_three, second_gain, second_up, second_down, second_kept, upstream
        )
        gain_sums[4] = gain_sums[4] + gain_part
        late[4] = late[4] + up_part
        late[5] = late[5] + down_part
        branch_grad = upstream.astype(jnp.bfloat16)
        late[3] = late[3] + inner_left(self_mixed, branch_grad)
        mixed_grad = (
            inner_right(branch_grad, self_output)
            .astype(jnp.bfloat16)
            .reshape(latent_rows, head_count, head_width)
        )
        probs_again = jnp.exp(
            head_scores(heads_query, heads_key, latent_ids, id_all, self_scale) - self_lse
        )
        prob_grad = jnp.einsum(
            "qhd,khd->hqk", mixed_grad, heads_value, preferred_element_type=jnp.float32
        )
        score_grad = (
            probs_again * (prob_grad - jnp.sum(probs_again * prob_grad, axis=2, keepdims=True))
        ).astype(jnp.bfloat16)
        query_grad = (
            jnp.einsum("hqk,khd->qhd", score_grad, heads_key, preferred_element_type=jnp.float32)
            * self_scale
        )
        query_grad = query_grad.reshape(latent_rows, width).astype(jnp.bfloat16)
        key_part = (
            jnp.einsum(
                "hqk,qhd->khd", score_grad, heads_query, preferred_element_type=jnp.float32
            ).reshape(-1, width)
            * self_scale
        )
        value_part = jnp.einsum(
            "hqk,qhd->khd",
            probs_again.astype(jnp.bfloat16),
            mixed_grad,
            preferred_element_type=jnp.float32,
        ).reshape(-1, width)
        key_grad, value_grad = (
            lax.psum_scatter(key_part, "row", scatter_dimension=0, tiled=True),
            lax.psum_scatter(value_part, "row", scatter_dimension=0, tiled=True),
        )
        key_grad = key_grad.astype(jnp.bfloat16)
        value_grad = value_grad.astype(jnp.bfloat16)
        late[0] = late[0] + inner_left(self_normed, query_grad)
        late[1] = late[1] + inner_left(self_normed, key_grad)
        late[2] = late[2] + inner_left(self_normed, value_grad)
        normed_grad = (
            inner_right(query_grad, self_query)
            + inner_right(key_grad, self_key)
            + inner_right(value_grad, self_value)
        )
        stream_grad, gain_part = norm_back(stream_two, self_gain, normed_grad)
        gain_sums[3] = gain_sums[3] + gain_part
        upstream = upstream + stream_grad
        upstream, gain_part, up_part, down_part = mlp_backward(
            stream_one, mlp_gain, up_weight, down_weight, first_kept, upstream
        )
        gain_sums[2] = gain_sums[2] + gain_part
        early[4] = early[4] + up_part
        early[5] = early[5] + down_part
        branch_grad = upstream.astype(jnp.bfloat16)
        early[3] = early[3] + inner_left(attended, branch_grad)
        attended_grad = inner_right(branch_grad, output_weight).astype(jnp.bfloat16)
        probs_full = jnp.exp(
            masked_scores(queries, all_keys, latent_ids, key_ids, cross_scale) - cross_lse
        )
        full_grad = inner_right(attended_grad, all_values)
        row_sums = jnp.sum(probs_full * full_grad, axis=1, keepdims=True)
        cross_grad = (probs_full * (full_grad - row_sums)).astype(jnp.bfloat16)
        cross_query_grad = (matmul(cross_grad, all_keys) * cross_scale).astype(jnp.bfloat16)
        probs_rounded = probs_full.astype(jnp.bfloat16)
        summed = lax.psum_scatter(
            jnp.concatenate(
                [
                    inner_left(cross_grad, queries) * cross_scale,
                    inner_left(probs_rounded, attended_grad),
                ],
                axis=1,
            ).astype(jnp.bfloat16),
            "row",
            scatter_dimension=0,
            tiled=True,
        ).astype(jnp.float32)
        own_key_grad = summed[:, :width].astype(jnp.bfloat16)
        own_value_grad = summed[:, width:].astype(jnp.bfloat16)
        early[1] = early[1] + inner_left(pixel_normed, own_key_grad)
        early[2] = early[2] + inner_left(pixel_normed, own_value_grad)
        pixel_normed_grad = inner_right(own_key_grad, key_weight) + inner_right(
            own_value_grad, value_weight
        )
        pixel_input_grad, gain_part = norm_back(pixel_float, pixel_gain, pixel_normed_grad)
        gain_sums[0] = gain_sums[0] + gain_part
        pixel_list.append(pixel_input_grad)
        early[0] = early[0] + inner_left(query_normed, cross_query_grad)
        query_input_grad, gain_part = norm_back(
            init_float, query_gain, inner_right(cross_query_grad, query_weight)
        )
        gain_sums[1] = gain_sums[1] + gain_part
        init_sum = init_sum + upstream + query_input_grad
    shards = (
        lax.psum_scatter(early[0], "seq", scatter_dimension=1, tiled=True),
        lax.psum_scatter(early[1], "seq", scatter_dimension=1, tiled=True),
        lax.psum_scatter(early[2], "seq", scatter_dimension=1, tiled=True),
        lax.psum_scatter(early[3], "seq", scatter_dimension=1, tiled=True),
        lax.psum_scatter(early[4], "seq", scatter_dimension=1, tiled=True),
        lax.psum_scatter(early[5], "seq", scatter_dimension=1, tiled=True),
        lax.psum_scatter(late[0], "seq", scatter_dimension=1, tiled=True),
        lax.psum_scatter(late[1], "seq", scatter_dimension=1, tiled=True),
        lax.psum_scatter(late[2], "seq", scatter_dimension=1, tiled=True),
        lax.psum_scatter(late[3], "seq", scatter_dimension=1, tiled=True),
        lax.psum_scatter(late[4], "seq", scatter_dimension=1, tiled=True),
        lax.psum_scatter(late[5], "seq", scatter_dimension=1, tiled=True),
        lax.psum_scatter(init_sum, "seq", scatter_dimension=1, tiled=True),
    )
    totals = (
        lax.psum(shards[0].astype(jnp.bfloat16), "row").astype(jnp.float32),
        lax.psum(shards[1].astype(jnp.bfloat16), "row").astype(jnp.float32),
        lax.psum(shards[2].astype(jnp.bfloat16), "row").astype(jnp.float32),
        lax.psum(shards[3].astype(jnp.bfloat16), "row").astype(jnp.float32),
        lax.psum(shards[4].astype(jnp.bfloat16), "row").astype(jnp.float32),
        lax.psum(shards[5].astype(jnp.bfloat16), "row").astype(jnp.float32),
        lax.psum(shards[6].astype(jnp.bfloat16), "row").astype(jnp.float32),
        lax.psum(shards[7].astype(jnp.bfloat16), "row").astype(jnp.float32),
        lax.psum(shards[8].astype(jnp.bfloat16), "row").astype(jnp.float32),
        lax.psum(shards[9].astype(jnp.bfloat16), "row").astype(jnp.float32),
        lax.psum(shards[10].astype(jnp.bfloat16), "row").astype(jnp.float32),
        lax.psum(shards[11].astype(jnp.bfloat16), "row").astype(jnp.float32),
    )
    early_done = totals[:6]
    late_done = totals[6:]
    init_total = shards[12]
    gain_total = lax.psum(
        (gain_sums[0], gain_sums[1], gain_sums[2], gain_sums[3], gain_sums[4]), ("seq", "row")
    )
    return (
        jnp.stack(latent_list),
        jnp.stack(pixel_list),
        init_total,
        gain_total[0],
        gain_total[1],
        gain_total[2],
        gain_total[3],
        gain_total[4],
        early_done[0],
        early_done[1],
        early_done[2],
        early_done[3],
        early_done[4],
        early_done[5],
        late_done[0],
        late_done[1],
        late_done[2],
        late_done[3],
        late_done[4],
        late_done[5],
    )


def solution(mesh):
    placed = (
        P("seq", "row", None),
        P("seq", "row"),
        P("seq", "row"),
        P("row", None),
        P("seq", "row", None),
        P(),
        P(),
        P(),
        P(),
        P(),
        P(),
        P(),
        P(),
        P(),
        P(),
        P(),
        P(),
        P(),
        P(),
        P(),
        P(),
        P(),
    )
    return jax.shard_map(
        body,
        mesh=mesh,
        in_specs=placed,
        out_specs=(
            P("seq", "row", None),
            P("seq", "row", None),
            P("row", "seq"),
            P(),
            P(),
            P(),
            P(),
            P(),
            P(None, "seq"),
            P(None, "seq"),
            P(None, "seq"),
            P(None, "seq"),
            P(None, "seq"),
            P(None, "seq"),
            P(None, "seq"),
            P(None, "seq"),
            P(None, "seq"),
            P(None, "seq"),
            P(None, "seq"),
            P(None, "seq"),
        ),
        check_vma=False,
    )
```

profile of v0, /device:TPU:0, one launch (start us, length us, event | category | flops | bytes accessed | tf_op | source)
XLA Modules:
  0.0 2442.2 jit_solution(5599507859738250607)
XLA Ops:
  56.6 73.6 %all-gather.21.cloned.1.call-done = bf16[8192,1024]{1,0:T(8,128)(2,1)} async-done(((bf16[2048,1024]{1,0:T(8,128)(2,1)}), bf16[8192,1024]{1,0:T(8,128)(2,1)}) %all-gather.21.cloned.1.call-update) | async-done | bytes 16777232 | tf_op jit(solution)/shard_map/all_gather | solution.py:135
  147.4 90.9 %all-gather.23.cloned.1.call-done = bf16[8192,1024]{1,0:T(8,128)(2,1)} async-done(((bf16[2048,1024]{1,0:T(8,128)(2,1)}), bf16[8192,1024]{1,0:T(8,128)(2,1)}) %all-gather.23.cloned.1.call-update) | async-done | bytes 16777232 | tf_op jit(solution)/shard_map/all_gather | solution.py:136
  252.9 92.9 %all-gather.13.cloned.1.call-done = bf16[8192,1024]{1,0:T(8,128)(2,1)} async-done(((bf16[2048,1024]{1,0:T(8,128)(2,1)}), bf16[8192,1024]{1,0:T(8,128)(2,1)}) %all-gather.13.cloned.1.call-update) | async-done | bytes 16777232 | tf_op jit(solution)/shard_map/all_gather | solution.py:135
  363.8 89.3 %all-gather.15.cloned.1.call-done = bf16[8192,1024]{1,0:T(8,128)(2,1)} async-done(((bf16[2048,1024]{1,0:T(8,128)(2,1)}), bf16[8192,1024]{1,0:T(8,128)(2,1)}) %all-gather.15.cloned.1.call-update) | async-done | bytes 16777232 | tf_op jit(solution)/shard_map/all_gather | solution.py:136
  599.1 30.6 %reduce-scatter.28.cloned.1.call-done = f32[128,1024]{0,1:T(8,128)} async-done(((f32[512,1024]{0,1:T(8,128)}), f32[128,1024]{0,1:T(8,128)}) %reduce-scatter.28.cloned.1.call-update) | async-done | bytes 524304 | tf_op jit(solution)/shard_map/reduce_scatter | solution.py:215
  633.1 30.5 %reduce-scatter.20.cloned.1.call-done = f32[128,1024]{0,1:T(8,128)} async-done(((f32[512,1024]{0,1:T(8,128)}), f32[128,1024]{0,1:T(8,128)}) %reduce-scatter.20.cloned.1.call-update) | async-done | bytes 524304 | tf_op jit(solution)/shard_map/reduce_scatter | solution.py:214
  666.5 31.2 %reduce-scatter.22.cloned.1.call-done = f32[128,1024]{0,1:T(8,128)} async-done(((f32[512,1024]{0,1:T(8,128)}), f32[128,1024]{0,1:T(8,128)}) %reduce-scatter.22.cloned.1.call-update) | async-done | bytes 524304 | tf_op jit(solution)/shard_map/reduce_scatter | solution.py:215
  833.1 23.3 pad_maximum_fusion
  926.2 86.3 %reduce-scatter.30.cloned.1.call-done = bf16[2048,2048]{0,1:T(8,128)(2,1)} async-done(((bf16[8192,2048]{0,1:T(8,128)(2,1)}), bf16[2048,2048]{0,1:T(8,128)(2,1)}) %reduce-scatter.30.cloned.1.call-update) | async-done | bytes 8388624 | tf_op jit(solution)/shard_map/reduce_scatter | solution.py:247
  1017.1 232.8 %reduce-scatter.24.cloned.1.call-done = bf16[2048,2048]{0,1:T(8,128)(2,1)} async-done(((bf16[8192,2048]{0,1:T(8,128)(2,1)}), bf16[2048,2048]{0,1:T(8,128)(2,1)}) %reduce-scatter.24.cloned.1.call-update) | async-done | bytes 8388624 | tf_op jit(solution)/shard_map/reduce_scatter | solution.py:247
  1270.6 71.1 %reduce-scatter.54.cloned.1.call-done = f32[1024,128]{1,0:T(8,128)} async-done(((f32[1024,1024]{1,0:T(8,128)}), f32[1024,128]{1,0:T(8,128)}) %reduce-scatter.54.cloned.1.call-update) | async-done | bytes 524304 | tf_op jit(solution)/shard_map/reduce_scatter | solution.py:286
  1343.5 90.2 %reduce-scatter.46.cloned.1.call-done = f32[1024,128]{1,0:T(8,128)} async-done(((f32[1024,1024]{1,0:T(8,128)}), f32[1024,128]{1,0:T(8,128)}) %reduce-scatter.46.cloned.1.call-update) | async-done | bytes 524304 | tf_op jit(solution)/shard_map/reduce_scatter | solution.py:282
  1435.5 90.0 %reduce-scatter.52.cloned.1.call-done = f32[1024,128]{1,0:T(8,128)} async-done(((f32[1024,1024]{1,0:T(8,128)}), f32[1024,128]{1,0:T(8,128)}) %reduce-scatter.52.cloned.1.call-update) | async-done | bytes 524304 | tf_op jit(solution)/shard_map/reduce_scatter | solution.py:285
  1527.2 90.2 %reduce-scatter.56.cloned.1.call-done = f32[1024,128]{1,0:T(8,128)} async-done(((f32[1024,1024]{1,0:T(8,128)}), f32[1024,128]{1,0:T(8,128)}) %reduce-scatter.56.cloned.1.call-update) | async-done | bytes 524304 | tf_op jit(solution)/shard_map/reduce_scatter | solution.py:287
  1619.2 90.1 %reduce-scatter.44.cloned.1.call-done = f32[1024,128]{1,0:T(8,128)} async-done(((f32[1024,1024]{1,0:T(8,128)}), f32[1024,128]{1,0:T(8,128)}) %reduce-scatter.44.cloned.1.call-update) | async-done | bytes 524304 | tf_op jit(solution)/shard_map/reduce_scatter | solution.py:281
  1711.1 90.4 %reduce-scatter.42.cloned.1.call-done = f32[1024,128]{1,0:T(8,128)} async-done(((f32[1024,1024]{1,0:T(8,128)}), f32[1024,128]{1,0:T(8,128)}) %reduce-scatter.42.cloned.1.call-update) | async-done | bytes 524304 | tf_op jit(solution)/shard_map/reduce_scatter | solution.py:280
  1803.3 90.1 %reduce-scatter.40.cloned.1.call-done = f32[1024,128]{1,0:T(8,128)} async-done(((f32[1024,1024]{1,0:T(8,128)}), f32[1024,128]{1,0:T(8,128)}) %reduce-scatter.40.cloned.1.call-update) | async-done | bytes 524304 | tf_op jit(solution)/shard_map/reduce_scatter | solution.py:279
  1895.2 90.5 %reduce-scatter.50.cloned.1.call-done = f32[1024,128]{1,0:T(8,128)} async-done(((f32[1024,1024]{1,0:T(8,128)}), f32[1024,128]{1,0:T(8,128)}) %reduce-scatter.50.cloned.1.call-update) | async-done | bytes 524304 | tf_op jit(solution)/shard_map/reduce_scatter | solution.py:284
  1987.5 90.1 %reduce-scatter.48.cloned.1.call-done = f32[1024,128]{1,0:T(8,128)} async-done(((f32[1024,1024]{1,0:T(8,128)}), f32[1024,128]{1,0:T(8,128)}) %reduce-scatter.48.cloned.1.call-update) | async-done | bytes 524304 | tf_op jit(solution)/shard_map/reduce_scatter | solution.py:283
  2079.4 91.0 %reduce-scatter.34.cloned.1.call-done = f32[1024,128]{1,0:T(8,128)} async-done(((f32[1024,1024]{1,0:T(8,128)}), f32[1024,128]{1,0:T(8,128)}) %reduce-scatter.34.cloned.1.call-update) | async-done | bytes 524304 | tf_op jit(solution)/shard_map/reduce_scatter | solution.py:276
  2172.2 63.2 %reduce-scatter.36.cloned.1.call-done = f32[261,128]{1,0:T(8,128)} async-done(((f32[261,1024]{1,0:T(8,128)}), f32[261,128]{1,0:T(8,128)}) %reduce-scatter.36.cloned.1.call-update) | async-done | bytes 133648 | tf_op jit(solution)/shard_map/reduce_scatter | solution.py:277
  2237.0 62.4 %reduce-scatter.38.cloned.1.call-done = f32[261,128]{1,0:T(8,128)} async-done(((f32[261,1024]{1,0:T(8,128)}), f32[261,128]{1,0:T(8,128)}) %reduce-scatter.38.cloned.1.call-update) | async-done | bytes 133648 | tf_op jit(solution)/shard_map/reduce_scatter | solution.py:278
  2323.7 40.4 %all-reduce = (f32[261]{0:T(512)}, f32[1024]{0:T(1024)}, f32[1024]{0:T(1024)}, f32[1024]{0:T(1024)}, f32[1024]{0:T(1024)}) all-reduce(f32[261]{0:T(512)S(1)} %add.363, f32[1024]{0:T(1024)S(1)} %add.364, f32[1024]{0:T(1024)S(1)} %add.365, f32[1024]{0:T(1024)S(1)} %add.366, ...), channel_id=1, replica_groups=mesh['seq'=8,'row'=4] {'seq','row'}, use_global_device_ids=true, to_apply=%region_59.60 | all-reduce | flops 4357 | bytes 34856 | tf_op jit(solution)/shard_map/psum | solution.py:307
  2381.7 53.4 %reduce-scatter.32.cloned.1.call-done = f32[128,128]{1,0:T(8,128)} async-done(((f32[128,1024]{1,0:T(8,128)}), f32[128,128]{1,0:T(8,128)}) %reduce-scatter.32.cloned.1.call-update) | async-done | bytes 65552 | tf_op jit(solution)/shard_map/reduce_scatter | solution.py:288
  (657 shorter events, 540.3 us)
Async XLA Ops:
  7.2 123.0 %all-gather.21.cloned.1.call-start = ((), (), s32[]{:S(2)}) async-start(), calls=%async_computation.23 | async-start | bytes 20971520 | tf_op jit(solution)/shard_map/all_gather | solution.py:135
  21.0 217.2 %all-gather.23.cloned.1.call-start = ((), (), s32[]{:S(2)}) async-start(), calls=%async_computation.24 | async-start | bytes 20971520 | tf_op jit(solution)/shard_map/all_gather | solution.py:136
  26.7 319.1 %all-gather.13.cloned.1.call-start = ((), (), s32[]{:S(2)}) async-start(), calls=%async_computation.19 | async-start | bytes 20971520 | tf_op jit(solution)/shard_map/all_gather | solution.py:135
  34.8 418.4 %all-gather.15.cloned.1.call-start = ((), (), s32[]{:S(2)}) async-start(), calls=%async_computation.20 | async-start | bytes 20971520 | tf_op jit(solution)/shard_map/all_gather | solution.py:136
  40.9 453.2 %all-gather.27.cloned.1.call-start = ((), (), s32[]{:S(2)}) async-start(), calls=%async_computation.26 | async-start | bytes 1310720 | tf_op jit(solution)/shard_map/all_gather | solution.py:153
  494.0 101.6 %reduce-scatter.26.cloned.1.call-start = ((), (), s32[]{:S(2)}) async-start(), calls=%async_computation.30 | async-start | bytes 2621440 | tf_op jit(solution)/shard_map/reduce_scatter | solution.py:214
  567.0 96.6 %reduce-scatter.20.cloned.1.call-start = ((), (), s32[]{:S(2)}) async-start(), calls=%async_computation.27 | async-start | bytes 2621440 | tf_op jit(solution)/shard_map/reduce_scatter | solution.py:214
  577.3 120.4 %reduce-scatter.22.cloned.1.call-start = ((), (), s32[]{:S(2)}) async-start(), calls=%async_computation.28 | async-start | bytes 2621440 | tf_op jit(solution)/shard_map/reduce_scatter | solution.py:215
  579.3 433.2 %reduce-scatter.30.cloned.1.call-start = ((), (), s32[]{:S(2)}) async-start(), calls=%async_computation.32 | async-start | bytes 41943040 | tf_op jit(solution)/shard_map/reduce_scatter | solution.py:247
  777.6 472.3 %reduce-scatter.24.cloned.1.call-start = ((), (), s32[]{:S(2)}) async-start(), calls=%async_computation.29 | async-start | bytes 41943040 | tf_op jit(solution)/shard_map/reduce_scatter | solution.py:247
  856.5 485.2 %reduce-scatter.54.cloned.1.call-start = ((), (), s32[]{:S(2)}) async-start(), calls=%async_computation.44 | async-start | bytes 4718592 | tf_op jit(solution)/shard_map/reduce_scatter | solution.py:286
  861.4 572.3 %reduce-scatter.46.cloned.1.call-start = ((), (), s32[]{:S(2)}) async-start(), calls=%async_computation.40 | async-start | bytes 4718592 | tf_op jit(solution)/shard_map/reduce_scatter | solution.py:282
  866.0 659.5 %reduce-scatter.52.cloned.1.call-start = ((), (), s32[]{:S(2)}) async-start(), calls=%async_computation.43 | async-start | bytes 4718592 | tf_op jit(solution)/shard_map/reduce_scatter | solution.py:285
  870.6 746.7 %reduce-scatter.56.cloned.1.call-start = ((), (), s32[]{:S(2)}) async-start(), calls=%async_computation.45 | async-start | bytes 4718592 | tf_op jit(solution)/shard_map/reduce_scatter | solution.py:287
  877.6 831.7 %reduce-scatter.44.cloned.1.call-start = ((), (), s32[]{:S(2)}) async-start(), calls=%async_computation.39 | async-start | bytes 4718592 | tf_op jit(solution)/shard_map/reduce_scatter | solution.py:281
  884.5 917.0 %reduce-scatter.42.cloned.1.call-start = ((), (), s32[]{:S(2)}) async-start(), calls=%async_computation.38 | async-start | bytes 4718592 | tf_op jit(solution)/shard_map/reduce_scatter | solution.py:280
  889.4 1004.0 %reduce-scatter.40.cloned.1.call-start = ((), (), s32[]{:S(2)}) async-start(), calls=%async_computation.37 | async-start | bytes 4718592 | tf_op jit(solution)/shard_map/reduce_scatter | solution.py:279
  894.2 1091.5 %reduce-scatter.50.cloned.1.call-start = ((), (), s32[]{:S(2)}) async-start(), calls=%async_computation.42 | async-start | bytes 4718592 | tf_op jit(solution)/shard_map/reduce_scatter | solution.py:284
  899.7 1177.9 %reduce-scatter.48.cloned.1.call-start = ((), (), s32[]{:S(2)}) async-start(), calls=%async_computation.41 | async-start | bytes 4718592 | tf_op jit(solution)/shard_map/reduce_scatter | solution.py:283
  904.7 1265.7 %reduce-scatter.34.cloned.1.call-start = ((), (), s32[]{:S(2)}) async-start(), calls=%async_computation.34 | async-start | bytes 4718592 | tf_op jit(solution)/shard_map/reduce_scatter | solution.py:276
  926.2 1309.2 %reduce-scatter.36.cloned.1.call-start = ((), (), s32[]{:S(2)}) async-start(), calls=%async_computation.35 | async-start | bytes 1216512 | tf_op jit(solution)/shard_map/reduce_scatter | solution.py:277
  1255.1 1044.3 %reduce-scatter.38.cloned.1.call-start = ((), (), s32[]{:S(2)}) async-start(), calls=%async_computation.36 | async-start | bytes 1216512 | tf_op jit(solution)/shard_map/reduce_scatter | solution.py:278
  1262.9 1105.3 %all-reduce.4.cloned.1.call-start = ((), (), s32[]{:S(2)}) async-start(), calls=%async_computation.46 | async-start | bytes 5513216 | tf_op jit(solution)/shard_map/psum | solution.py:291
  2300.9 134.2 %reduce-scatter.32.cloned.1.call-start = ((), (), s32[]{:S(2)}) async-start(), calls=%async_computation.33 | async-start | bytes 589824 | tf_op jit(solution)/shard_map/reduce_scatter | solution.py:288
  (190 other events, 4856.2 us)
Sparse Core Ops, SparseCore 0:
  21.2 108.9 all-gather.20
  132.3 105.9 all-gather.22
  239.8 105.9 all-gather.12
  347.3 105.8 all-gather.14
  564.1 31.4 reduce-scatter.25
  598.1 31.4 reduce-scatter.27
  632.2 31.4 reduce-scatter.19
  666.2 31.4 reduce-scatter.21
  777.7 234.8 reduce-scatter.29
  1015.0 234.8 reduce-scatter.23
  1253.3 88.3 reduce-scatter.53
  1345.6 88.0 reduce-scatter.45
  1437.2 88.2 reduce-scatter.51
  1529.4 87.9 reduce-scatter.55
  1621.0 88.2 reduce-scatter.43
  1713.2 88.2 reduce-scatter.41
  1805.1 88.2 reduce-scatter.39
  1897.5 88.2 reduce-scatter.49
  1989.4 88.2 reduce-scatter.47
  2082.1 88.2 reduce-scatter.33
  2173.8 61.5 reduce-scatter.35
  2238.7 60.6 reduce-scatter.37
  2303.7 64.5 all-reduce.3
  2372.5 62.5 reduce-scatter.31
  (4 shorter events, 66.7 us)
where the time goes:
time: 2450 us; the launch traced here: 2440 us
  waiting for transfers between devices  1860 us (76%)
  matrix products  336 us (14%)
  other arithmetic  118 us (5%)
  blocking collectives  62.3 us (3%)
  local copies, waits for them, and re-layouts  44.8 us (2%)
    reduce_scatter x2, waiting for transfers between devices, body(): lax.psum_scatter(jnp.concatenate([inner_left(cross_grad, queries) * cross...  319 us
    all_gather x2, waiting for transfers between devices, body(): lax.all_gather(own_values, 'row', axis=0, tiled=True)  180 us
    all_gather x2, waiting for transfers between devices, body(): lax.all_gather(own_keys, 'row', axis=0, tiled=True)  167 us
    dot_general x28, matrix products, inner_right(): lax.dot_general(former, latter, (((1,), (1,)), ((), ())), preferred_eleme...  113 us
    dot_general x28, matrix products, inner_left(): lax.dot_general(former, latter, (((0,), (0,)), ((), ())), preferred_eleme...  111 us
    reduce_scatter x1, waiting for transfers between devices, body(): lax.psum_scatter(early[0], 'seq', scatter_dimension=1, tiled=True)  91 us
    reduce_scatter x1, waiting for transfers between devices, body(): lax.psum_scatter(late[2], 'seq', scatter_dimension=1, tiled=True)  90.5 us
    reduce_scatter x1, waiting for transfers between devices, body(): lax.psum_scatter(early[4], 'seq', scatter_dimension=1, tiled=True)  90.4 us
  transfers between devices with their start and end apart: 28, of which 27 were waited for; matrix products, arithmetic and copies ran while one was open for 14% of the time, Pallas kernels for 0%

commit v1 on v0

v1 whole, which is shorter than its diff:
```python
import functools
import math

import jax
import jax.numpy as jnp
from jax import lax
from jax.experimental import pallas as pl
from jax.experimental.pallas import tpu as pltpu
from jax.sharding import PartitionSpec as P

HEADS = 8
EPSILON = 1e-05
NEGATIVE = -1e9
BF = jnp.bfloat16
F32 = jnp.float32
LANES = 128
FEAT_PAD = 384
MAIN = 256
CAT = 2 * MAIN + LANES
MESH = pl.DeviceIdType.MESH


def dot(a, b):
    return jnp.dot(a, b, preferred_element_type=F32)


def dot_tn(a, b):
    return lax.dot_general(a, b, (((0,), (0,)), ((), ())), preferred_element_type=F32)


def dot_nt(a, b):
    return lax.dot_general(a, b, (((1,), (1,)), ((), ())), preferred_element_type=F32)


def fill_rest(rest, matrix):
    rest[...] = jnp.zeros(rest.shape, rest.dtype)
    rest[: matrix.shape[0] - MAIN, :] = matrix[MAIN:, :]


def norm_parts(values):
    centre = values - jnp.mean(values, axis=-1, keepdims=True)
    rs = lax.rsqrt(jnp.mean(centre * centre, axis=-1, keepdims=True) + EPSILON)
    return centre * rs, rs


def norm_back(unit, rs, gain, upstream):
    scaled = upstream * gain
    grad = rs * (
        scaled
        - jnp.mean(scaled, axis=-1, keepdims=True)
        - unit * jnp.mean(scaled * unit, axis=-1, keepdims=True)
    )
    return grad, jnp.sum(upstream * unit, axis=0)


def gelu_parts(hidden):
    cdf = 0.5 * (1.0 + lax.erf(hidden * math.sqrt(0.5)))
    pdf = jnp.exp(-0.5 * hidden * hidden) * (1.0 / math.sqrt(2.0 * math.pi))
    return hidden * cdf, cdf + hidden * pdf


NORMED1, ACTIVE1, SELFN, MIXED, NORMED2, ACTIVE2 = range(6)
DOWN2, UP2, SOUT, SQ, SK, SV, DOWN1, UP1 = range(8)
LEFT = {
    DOWN2: ACTIVE2, UP2: NORMED2, SOUT: MIXED, SQ: SELFN, SK: SELFN, SV: SELFN,
    DOWN1: ACTIVE1, UP1: NORMED1,
}
MATS = 8
FEATURE_UNIT = 2 * MATS
INIT_UNIT = FEATURE_UNIT + 1
UNITS = INIT_UNIT + 1


class Remote:
    def __init__(self, log, src, dst, send_sem, recv_sem, device):
        self.copy = pltpu.make_async_remote_copy(
            src_ref=src, dst_ref=dst, send_sem=send_sem, recv_sem=recv_sem,
            device_id=device, device_id_type=MESH,
        )
        self.copy.start()
        self.arrived = self.sent = False
        log.append(self)

    def wait_recv(self):
        if not self.arrived:
            self.copy.wait_recv()
        self.arrived = True

    def wait_send(self):
        if not self.sent:
            self.copy.wait_send()
        self.sent = True

    def finish(self):
        self.wait_recv()
        self.wait_send()


def unit_orders(bits):
    rest = list(range(bits))
    head, tail = rest[:2], rest[2:]
    by_y = ["y"] + rest
    by_first = head + ["y"] + tail
    by_second = head[::-1] + ["y"] + tail
    kinds = [by_y, by_first, by_second]
    return [kinds[u % 3] for u in range(UNITS)]


def stage_shapes(order, width):
    shapes, planes, size = [], 2, width
    for axis in order:
        if axis == "y":
            planes = 1
            shapes.append((size, LANES))
        else:
            size //= 2
            shapes.append((2, size, LANES) if planes == 2 else (size, LANES))
    return shapes


def main_kernel(cfg, *refs):
    shards, width, count, sizes = cfg
    bits = shards.bit_length() - 1
    share = width // shards
    half = width // 2
    block = count // 2
    lat = 2 * count
    head_width = width // HEADS
    cross_scale = 1.0 / math.sqrt(width)
    self_scale = 1.0 / math.sqrt(head_width)
    orders = unit_orders(bits)
    it = iter(refs)

    def take(n=None):
        return next(it) if n is None else [next(it) for _ in range(n)]

    (z_hbm, pixel_gain, pseg_ref, init_ref, cot_hbm, seg_ref, wk_hbm, wv_hbm) = take(8)
    gain_refs = take(4)
    w_hbm = take(10)
    (lat_ref, sm_out, gat_ref, initg_ref, fold, zall, y_ref, pspill) = take(8)
    (wslots, wkv, w_rest, zbuf, ain1, asum, ain2, amix, amix_in, amat, fbuf, rsb, acts, acts_in, slopes,
     qbuf, kv, pbuf, dmix, dkv_in, gall, gcd_in, fin, da_all, bsum, gsum, idrow,
     sm, xcat, flat, rest0, pixel_rs, gain_col, fin_in, part) = take(35)
    recv = [take(len(orders[u])) for u in range(UNITS)]
    smr = take(sizes["small_stages"])
    (wsem, zsem, usend, urecv, csend, crecv) = take(6)

    j = lax.axis_index("seq")
    row = lax.axis_index("row")
    core, chip = row % 2, row // 2
    peer = {"row": row + 1 - 2 * core}
    across = {"row": row + 2 - 4 * chip}
    diagonal = {"row": 3 - row}
    bit_of = [(j // (1 << b)) % 2 for b in range(bits)]
    partner = {b: {"seq": j + (1 - 2 * bit_of[b]) * (1 << b)} for b in range(bits)}
    partner["y"] = across
    stream = fbuf.at[pl.ds(0, count)]
    upstr = fbuf.at[pl.ds(count, count)]
    dnorm = stream

    def act(k):
        return pl.ds(k * count, count)

    WQ, WO, UP, DOWN, QW, KW, VW, SO, UPB, DOWNB = range(10)
    uses = [WQ, WO, UP, DOWN, KW, VW, QW, SO, UPB, DOWNB, DOWNB, UPB, SO, QW, KW, VW, DOWN, UP, WO]
    nslots = wslots.shape[0]
    at_use = [0]

    def weight_copy(i):
        return pltpu.make_async_copy(w_hbm[uses[i]], wslots.at[i % nslots], wsem.at[i % nslots])

    def weight(expect):
        i = at_use[0]
        assert uses[i] == expect
        at_use[0] += 1
        weight_copy(i).wait()
        return wslots.at[i % nslots]

    def weight_done():
        i = at_use[0] - 1 + nslots
        if i < len(uses):
            weight_copy(i).start()

    features = wk_hbm.shape[0]
    pixel_copies = []
    for i, lo in enumerate(range(0, z_hbm.shape[0], width)):
        rows = min(width, z_hbm.shape[0] - lo)
        pixel_copies.append(pltpu.make_async_copy(
            z_hbm.at[pl.ds(lo, rows)], part.at[i, pl.ds(0, rows)], zsem.at[i]
        ))
    weight_copy(0).start()
    wk_copy = pltpu.make_async_copy(wk_hbm, wkv, wsem.at[nslots])
    wk_copy.start()
    for i in range(1, nslots):
        weight_copy(i).start()
    wv_copy = pltpu.make_async_copy(wv_hbm, wkv, wsem.at[nslots + 1])
    for copy in pixel_copies:
        copy.start()

    barrier = pltpu.get_barrier_semaphore()
    partners = [peer, across, diagonal] + [partner[b] for b in range(bits)]
    for p in partners:
        pl.semaphore_signal(barrier, inc=1, device_id=p, device_id_type=MESH)
    copies = []
    slot_count = [0]

    def remote(src, dst, device):
        slot = slot_count[0]
        slot_count[0] += 1
        return Remote(copies, src, dst, csend.at[slot], crecv.at[slot], device)

    def local(src, dst, slot):
        copy = pltpu.make_async_copy(src, dst, wsem.at[nslots + 2 + slot])
        copy.start()
        return copy

    def rows_loop(body, step=64, total=None):
        def run(i, carry):
            body(pl.ds(pl.multiple_of(i * step, step), step))
            return carry
        lax.fori_loop(0, (total or count) // step, run, 0, unroll=2)

    def columns_loop(body, step=256, total=width):
        def run(i, carry):
            body(pl.ds(pl.multiple_of(i * step, step), step))
            return carry
        lax.fori_loop(0, total // step, run, 0, unroll=2)

    def layer(k, into):
        def body(rows):
            unit, rs = norm_parts(stream[rows, :])
            rsb[k, rows, :] = jnp.broadcast_to(rs, (rs.shape[0], LANES))
            place = pl.ds(pl.multiple_of(into * count + rows.start, rows.size), rows.size)
            acts[place, :] = (unit * gain_refs[k][...]).astype(BF)
        rows_loop(body)

    def layer_back(k, normed, into, start=None):
        gain = gain_refs[k][...]
        inverse = 1.0 / gain

        def body(i, total):
            rows = pl.ds(pl.multiple_of(i * 64, 64), 64)
            place = pl.ds(pl.multiple_of(normed * count + i * 64, 64), 64)
            dn = dnorm[rows, :]
            unit = acts[place, :].astype(F32) * inverse
            scaled = dn * gain
            rs = rsb[k, rows, :][:, :1]
            mean = jnp.mean(scaled, axis=-1, keepdims=True)
            along = jnp.mean(scaled * unit, axis=-1, keepdims=True)
            before = upstr[rows, :] if start is None else gall[start, 0, rows, :].astype(F32)
            after = before + rs * (scaled - mean - unit * along)
            upstr[rows, :] = after
            gall[into, 0, rows, :] = after.astype(BF)
            return total + jnp.sum(dn * unit, axis=0, keepdims=True)
        gsum[pl.ds(k, 1), :] = lax.fori_loop(
            0, count // 64, body, jnp.zeros((1, width), F32), unroll=2
        )

    act_copies, grad_copies = {}, {}

    def share_act(k):
        away = pl.ds(pl.multiple_of((1 - core) * half, half), half)
        act_copies[k] = remote(acts.at[act(k), away], acts_in.at[k], peer)

    def share_grad(m):
        grad_copies[m] = remote(gall.at[m, 0], gall.at[m, 1], peer)

    clock = [0.0]
    small = dict(lo=0, size=lat, stage=0, up=[], copy=None, due=1e9)
    axes = [(core, peer), (chip, across)] + [(bit_of[b], partner[b]) for b in range(bits)]

    def small_send():
        bit, device = axes[small["stage"]]
        size = small["size"]
        if size > 16:
            size //= 2
            away = pl.multiple_of(small["lo"] + (1 - bit) * size, 16)
            keep = pl.multiple_of(small["lo"] + bit * size, 16)
            small["up"].append((device, keep, size))
            small["lo"], small["size"] = keep, size
        else:
            away = small["lo"]
        small["copy"] = remote(sm.at[pl.ds(away, size)], smr[small["stage"]], device)
        small["due"] = clock[0] + 2.5 + size * 512 * 4 / 75e3

    def small_grow():
        device, lo, size = small["up"].pop()
        rows = pl.ds(lo, size)
        small["copy"] = remote(sm_out.at[rows], sm_out.at[rows], device)
        small["due"] = clock[0] + 2.5 + size * 512 * 4 / 75e3

    def small_step():
        copy, size = small["copy"], small["size"]
        copy.wait_recv()
        if small["stage"] < len(axes):
            copy.wait_send()
            rows = pl.ds(small["lo"], size)
            sm[rows, :] = sm[rows, :] + smr[small["stage"]][...]
            small["stage"] += 1
            if small["stage"] < len(axes):
                small_send()
                return
            sm_out[rows, :] = sm[rows, :]
        if small["up"]:
            small_grow()
        else:
            small["due"] = 1e9

    state = {}
    free = {}
    pending = []

    def region(u, planes, lo, size):
        if planes == 2:
            return part.at[pl.ds(2 * u, 2), pl.ds(lo, size)]
        return part.at[2 * u + chip, pl.ds(lo, size)]

    def send_stage(u):
        s = state[u]
        axis = orders[u][s["stage"]]
        k = s["stage"]
        if axis == "y":
            src = part.at[2 * u + 1 - chip, pl.ds(s["lo"], s["size"])]
            s["planes"] = 1
        else:
            size = s["size"] // 2
            keep = s["lo"] + bit_of[axis] * size
            away = s["lo"] + (1 - bit_of[axis]) * size
            src = region(u, s["planes"], pl.multiple_of(away, share), size)
            s["lo"], s["size"] = pl.multiple_of(keep, share), size
        slot = sum(len(orders[v]) for v in range(u)) + k
        s["copy"] = Remote(copies, src, recv[u][k], usend.at[slot], urecv.at[slot], partner[axis])
        link = {"y": "y", 0: "x"}.get(axis, "z%s" % axis)
        begin = max(clock[0], free.get(link, 0.0))
        took = s["size"] * s["planes"] * LANES * 2 * (2 if link in ("x", "y", "z1") else 4) / 75e3
        free[link] = begin + took
        s["due"] = begin + took + 4.0
        pending.append(u)

    def finish_stage(u):
        s = state[u]
        k = s["stage"]
        s["copy"].wait_recv()
        last = k == len(orders[u]) - 1
        if last:
            total = part[pl.ds(2 * u + chip, 1), pl.ds(s["lo"], s["size"])][0] + recv[u][k][...]
            if u == INIT_UNIT:
                initg_ref[...] = total
            else:
                fin[u] = total
            s["done"] = True
            done_units.append(u)
            gather_ready()
            return
        step = min(s["size"], 256)
        for p in range(s["planes"]):
            def add(i, carry):
                off = pl.multiple_of(i * step, step)
                mine = pl.ds(pl.multiple_of(s["lo"] + off, share), step)
                if s["planes"] == 2:
                    got = recv[u][k][p, pl.ds(off, step), :]
                    part[2 * u + p, mine, :] = part[2 * u + p, mine, :] + got
                else:
                    got = recv[u][k][pl.ds(off, step), :]
                    at = pl.ds(2 * u + chip, 1)
                    part[at, mine, :] = part[at, mine, :] + got[None]
                return carry
            lax.fori_loop(0, s["size"] // step, add, 0)
        s["stage"] += 1
        send_stage(u)

    done_units, gathers = [], []
    groups = [list(range(0, 6)), list(range(6, 12)), list(range(12, FEATURE_UNIT + 1))]

    def gather_ready():
        while len(gathers) < len(groups) and all(u in done_units for u in groups[len(gathers)]):
            g = groups[len(gathers)]
            span = pl.ds(g[0], len(g))
            from_chip = remote(fin.at[span], fin_in.at[span], across)
            remote(fin.at[span], gat_ref.at[row, span], peer)
            gathers.append((g, from_chip, local(fin.at[span], gat_ref.at[row, span], len(gathers))))

    def serve():
        at = min((state[u]["due"], u) for u in pending) if pending else (1e9, None)
        if small["due"] <= at[0]:
            clock[0] = max(clock[0], small["due"])
            small_step()
        else:
            clock[0] = max(clock[0], at[0]) + 0.3
            pending.remove(at[1])
            finish_stage(at[1])

    def next_due():
        return min([small["due"]] + [state[u]["due"] for u in pending])

    def tick(us):
        clock[0] += 1.6 * us
        while next_due() <= clock[0]:
            serve()

    def begin_unit(u):
        state[u] = dict(stage=0, planes=2, lo=0, size=width, done=False)
        send_stage(u)

    def position(u, block):
        seq_bits = [a for a in orders[u] if a != "y"]
        pos = 0
        for at, b in enumerate(seq_bits):
            pos = pos + ((block // (1 << b)) % 2) * (1 << (bits - 1 - at))
        return pos

    def store_plane(u, plane, value):
        if share != LANES:
            value = value.astype(F32).T.astype(BF)
        for block_at in range(shards):
            place = pl.ds(position(u, block_at) * share, share)
            if share == LANES:
                part[pl.ds(2 * u + plane, 1), place, :] = value[:, block_at * share : (block_at + 1) * share][None]
            else:
                part[pl.ds(2 * u + plane, 1), place, :] = value[block_at * share : (block_at + 1) * share][None]

    def weight_grad(m):
        left = LEFT[m]
        act_copies[left].wait_recv()
        grad_copies[m].wait_recv()

        def run(plane, carry):
            own = pl.ds(pl.multiple_of(core * half + plane * MAIN, MAIN), MAIN)
            theirs = pl.ds(pl.multiple_of(plane * MAIN, MAIN), MAIN)
            lefts = jnp.concatenate([acts[act(left), own], acts_in[left, :, theirs]], axis=0)
            total = dot_tn(lefts, gall[m].reshape(2 * count, width)).astype(BF)
            store_plane(2 * m, plane, total[:LANES])
            store_plane(2 * m + 1, plane, total[LANES:])
            return carry
        lax.fori_loop(0, 2, run, 0)
        begin_unit(2 * m)
        begin_unit(2 * m + 1)

    cot_rows = pl.ds(pl.multiple_of(chip * block, block), block)
    c_own = local(cot_hbm.at[chip], gall.at[DOWN2, 0, cot_rows], 3)
    zbuf[pl.ds(chip, 1)] = init_ref[...][None]
    unit, unused = norm_parts(init_ref[...].astype(F32))
    own_normed = (unit * gain_refs[3][...]).astype(BF)
    w = weight(WQ)
    queries = dot(own_normed, w[...]).astype(BF)
    weight_done()
    wk_copy.wait()
    fill_rest(w_rest, wkv)
    fold_main = dot_nt(queries, wkv[:MAIN, :]) * cross_scale
    fold_rest = dot_nt(queries, w_rest[...]) * cross_scale
    own_rows = pl.ds(pl.multiple_of(row * block, block), block)
    seg = seg_ref[...].astype(F32)
    ids = jnp.concatenate([seg, jnp.zeros((LANES - 2, block), F32)], axis=0).T
    ids = pltpu.roll(ids, 5, 1)
    fold[own_rows, :MAIN] = fold_main.astype(BF)
    fold[own_rows, MAIN:] = (fold_rest + ids).astype(BF)
    wv_copy.start()
    pl.semaphore_wait(barrier, len(partners))
    fold_copies = [remote(fold.at[own_rows], fold.at[own_rows], p) for p in (across, diagonal, peer)]
    z_copy = remote(init_ref, zbuf.at[chip], across)
    c_copy = remote(cot_hbm.at[1 - chip], gall.at[DOWN2, 0, cot_rows], across)
    group = pixel_rs.shape[0]
    blocks = group // 4
    tall = gain_col.shape[0]

    fold_in = width // group

    def pixel_row(f, lo=0, rows=group):
        at = pl.ds(pl.multiple_of((f % fold_in) * group + lo, rows), rows)
        return part[pl.ds(f // fold_in, 1), at, :][0].astype(F32)

    zero = jnp.zeros((group, LANES), F32)
    for copy in pixel_copies:
        copy.wait()
    mean = lax.fori_loop(0, features, lambda f, acc: acc + pixel_row(f), zero, unroll=9)
    mean = mean * (1.0 / features)

    def spread(f, acc):
        centre = pixel_row(f) - mean
        return acc + centre * centre
    spread_sum = lax.fori_loop(0, features, spread, zero, unroll=9)
    rs_all = lax.rsqrt(spread_sum * (1.0 / features) + EPSILON)
    pixel_rs[...] = rs_all
    gain_col[...] = jnp.ones(gain_col.shape, F32)
    flat[features * group // 2 :, :] = jnp.zeros(((tall - features) * group // 2, LANES), F32)
    for s in range(2):
        xcat[s, 2 * MAIN + 16 :, :] = jnp.zeros((LANES - 16, xcat.shape[2]), BF)
    for k in range(2):
        half_rows = slice(k * (group // 2), (k + 1) * (group // 2))
        half_mean, half_rs = mean[half_rows], rs_all[half_rows]

        def scale(f, carry, k=k, half_mean=half_mean, half_rs=half_rs):
            value = pixel_row(f, k * (group // 2), group // 2)
            rows = pl.ds(pl.multiple_of(f * (group // 2), group // 2), group // 2)
            flat[rows, :] = (value - half_mean) * (half_rs * pixel_gain[f])
            if k == 0:
                gain_col[pl.ds(f, 1), :] = jnp.full((1, LANES), pixel_gain[f], F32)
            return carry
        lax.fori_loop(0, features, scale, 0, unroll=9)
        for s in range(2):
            for jb in range(blocks):
                cols = pl.ds(jb * LANES, LANES)
                value = flat[pl.ds(2 * jb + s, tall, stride=group // 2), :]
                xcat[s, k * MAIN : (k + 1) * MAIN, cols] = value[:MAIN].astype(BF)
                if k == 0:
                    rest0[s, :, cols] = value[MAIN:]
                else:
                    both = jnp.concatenate([rest0[s, :, cols], value[MAIN:]], axis=0)
                    xcat[s, 2 * MAIN : 2 * MAIN + 16, cols] = both.astype(BF)
    for copy in fold_copies:
        copy.wait_recv()

    lane = lax.broadcasted_iota(jnp.int32, (1, LANES), 1)
    image = (2 * row).astype(F32)

    def selectors(s, rows):
        ids = fold[rows, MAIN:].astype(F32)
        ids = jnp.where(s == 0, ids[:, 5:6], ids[:, 6:7])
        return jnp.where(ids == image, 1.0, 0.0), jnp.where(ids == image + 1.0, 1.0, 0.0)

    def spread_out(source, s, rows):
        first, second = selectors(s, rows)
        main = source[:, :MAIN].astype(F32)
        rest = jnp.where(lane < 5, source[:, MAIN:].astype(F32), 0.0)
        rest = rest * first + pltpu.roll(rest, 8, 1) * second
        return jnp.concatenate([main * first, main * second, rest], axis=1).astype(BF)

    def pull_in(s, rows, zero, one, rest):
        first, second = selectors(s, rows)
        rest = jnp.where(lane < 5, rest * first + pltpu.roll(rest, LANES - 8, 1) * second, 0.0)
        return zero * first + one * second, rest

    slots = xcat.shape[2]
    core_copies = []

    def send_core(turn):
        core_copies.append(remote(amat.at[turn, :, 1 - core], ain1.at[turn], peer))

    def core_sum(turn):
        core_copies[turn].wait_recv()
        return amat[turn, :, pl.ds(core, 1)][:, 0] + ain1[turn]

    for turn in range(2):
        s = 1 - chip if turn == 0 else chip
        seq = pl.ds(s, 1)
        for i in range(4):
            rows = pl.ds(i * block, block)
            gall[2 + 2 * turn + i // 2, 0, (i % 2) * block : (i % 2 + 1) * block, :CAT] = spread_out(
                fold[rows, :], s, rows
            )
        first_ok = jnp.where(pseg_ref[seq, :slots] == 2 * row, 1.0, 0.0)
        second_ok = jnp.where(pseg_ref[seq, slots:] == 2 * row + 1, 1.0, 0.0)

        def score_cols(cols, seq=seq, turn=turn):
            queries_cat = jnp.concatenate(
                [gall[2 + 2 * turn, 0, :, :CAT], gall[3 + 2 * turn, 0, :, :CAT]], axis=0
            )
            fbuf[:, cols] = dot(queries_cat, xcat[seq, :, cols][0])
        columns_loop(score_cols, 256, slots)
        if turn == 1:
            asum[...] = core_sum(0)
            step2 = remote(asum, ain2, across)

        def soften(rows, s=s, seq=seq, first_ok=first_ok, second_ok=second_ok):
            first, unused = selectors(s, rows)
            allowed = second_ok + first * (first_ok - second_ok)
            scores = jnp.where(allowed > 0.5, fbuf[rows, :], NEGATIVE)
            weights = jnp.exp(scores - jnp.max(scores, axis=1, keepdims=True))
            prob = (weights * (1.0 / jnp.sum(weights, axis=1, keepdims=True))).astype(BF)
            pbuf[seq, rows, :] = prob[None]
        rows_loop(soften, 64, lat)
        probs = pbuf[seq][0]
        zero = dot_nt(probs, xcat[seq, :MAIN, :][0])
        one = dot_nt(probs, xcat[seq, MAIN : 2 * MAIN, :][0])
        rest = dot_nt(probs, xcat[seq, 2 * MAIN :, :][0])
        main, rest = pull_in(s, pl.ds(0, lat), zero, one, rest)
        amat[turn, :, :, :, :MAIN] = main.astype(BF).reshape(2, 2, block, MAIN)
        amat[turn, :, :, :, MAIN:] = rest.astype(BF).reshape(2, 2, block, LANES)
        send_core(turn)
    spill = local(pbuf, pspill, 4)

    for at in range(4):
        who = core if at < 2 else 1 - core
        rows = pl.ds(pl.multiple_of((2 * (at % 2) + who) * block, block), block)
        turned = fold[rows, MAIN:].astype(F32).T
        idrow[:, at * block : (at + 1) * block] = jnp.where(chip == 0, turned[5:6], turned[6:7])
    own_ids = []
    for h in range(2):
        rows = pl.ds(pl.multiple_of((2 * h + core) * block, block), block)
        ids = fold[rows, MAIN:].astype(F32)
        own_ids.append(jnp.where(chip == 0, ids[:, 5:6], ids[:, 6:7]))
    idcol = jnp.concatenate(own_ids, axis=0)
    z_copy.wait_recv()
    remote(init_ref, zall.at[row], peer)
    other_row = row + 2 - 4 * chip
    remote(zbuf.at[1 - chip], zall.at[other_row], peer)
    z_local = [local(init_ref, zall.at[row], 5), local(zbuf.at[1 - chip], zall.at[other_row], 6)]
    c_copy.wait_recv()
    c_own.wait()
    share_grad(DOWN2)
    wv_copy.wait()
    fill_rest(w_rest, wkv)
    step2.wait_recv()
    amix[...] = (core_sum(1) + ain2[...]).reshape(count, FEAT_PAD)
    amix_copy = remote(amix, amix_in, peer)

    def attended_cols(cols):
        value = dot(amix[:, :MAIN], wkv[:MAIN, cols]) + dot(amix[:, MAIN:], w_rest[:, cols])
        qbuf[:, cols] = value.astype(BF)
    columns_loop(attended_cols)
    w = weight(WO)

    def one_cols(cols):
        start = zbuf[:, :, cols].reshape(count, cols.size).astype(F32)
        stream[:, cols] = start + dot(qbuf[...], w[:, cols])
    columns_loop(one_cols)
    weight_done()

    def mlp(k, normed, active, up_id, down_id):
        layer(k, normed)
        share_act(normed)
        w_up = weight(up_id)

        def up_cols(cols):
            value, slope = gelu_parts(dot(acts[act(normed), :], w_up[:, cols]))
            acts[act(active), cols] = value.astype(BF)
            slopes[active // 4, :, cols] = slope.astype(BF)
        columns_loop(up_cols)
        weight_done()
        share_act(active)
        w_down = weight(down_id)

        def down_cols(cols):
            stream[:, cols] += dot(acts[act(active), :], w_down[:, cols])
        columns_loop(down_cols)
        weight_done()

    mlp(0, NORMED1, ACTIVE1, UP, DOWN)
    layer(1, SELFN)
    share_act(SELFN)
    kv_copies = {}
    for index, dst in ((KW, 0), (VW, 1), (QW, None)):
        w_now = weight(index)

        def project(cols, dst=dst, w_now=w_now):
            value = dot(acts[act(SELFN), :], w_now[:, cols]).astype(BF)
            if dst is None:
                qbuf[:, cols] = value
            else:
                kv[dst, 0, :, cols] = value
        columns_loop(project)
        weight_done()
        if dst is not None:
            kv_copies[dst] = remote(kv.at[dst, 0], kv.at[dst, 1], peer)
    spill.wait()
    kv_copies[0].wait_recv()
    kv_copies[1].wait_recv()

    def heads(body):
        def run(pair, carry):
            for side in range(2):
                cols = pl.ds(pl.multiple_of((2 * pair + side) * head_width, head_width), head_width)
                rows = pl.ds(pl.multiple_of((pair % 2) * count, count), count)
                body(cols, (pl.ds(pair // 2, 1), rows, pl.ds(side * lat, lat)))
            return carry
        lax.fori_loop(0, HEADS // 2, run, 0)

    def attend(cols, keep):
        keys = kv[0, :, :, cols].reshape(lat, head_width)
        values = kv[1, :, :, cols].reshape(lat, head_width)
        scores = dot_nt(qbuf[:, cols], keys) * self_scale
        scores = jnp.where(idcol == idrow[...], scores, NEGATIVE)
        weights = jnp.exp(scores - jnp.max(scores, axis=1, keepdims=True))
        prob = (weights * (1.0 / jnp.sum(weights, axis=1, keepdims=True))).astype(BF)
        pbuf[keep] = prob[None]
        acts[act(MIXED), cols] = dot(prob, values).astype(BF)
    heads(attend)
    share_act(MIXED)
    w_so = weight(SO)

    def three_cols(cols):
        stream[:, cols] += dot(acts[act(MIXED), :], w_so[:, cols])
    columns_loop(three_cols)
    weight_done()
    mlp(2, NORMED2, ACTIVE2, UPB, DOWNB)
    dmix[...] = stream[...].astype(BF)
    lat_ref[pl.ds(chip, 1)] = dmix[pl.ds(pl.multiple_of(chip * block, block), block), :][None]
    lat_copy = remote(
        dmix.at[pl.ds(pl.multiple_of((1 - chip) * block, block), block)], lat_ref.at[chip], across
    )

    weight_grad(DOWN2)
    tick(2.0)

    def mlp_back(k, normed, active, m_down, m_up, up_id, down_id, into, start=None):
        w_down = weight(down_id)

        def act_cols(cols):
            grad = dot_nt(gall[m_down, 0], w_down[cols, :]).astype(BF).astype(F32)
            gall[m_up, 0, :, cols] = (grad * slopes[active // 4, :, cols].astype(F32)).astype(BF)
        columns_loop(act_cols)
        weight_done()
        share_grad(m_up)
        tick(1.0)
        w_up = weight(up_id)

        def norm_cols(cols):
            dnorm[:, cols] = dot_nt(gall[m_up, 0], w_up[cols, :])
        columns_loop(norm_cols)
        weight_done()
        if into == 0:
            grad_copies[DOWN2].wait_send()
            grad_copies[UP2].wait_send()
        layer_back(k, normed, into, start)
        tick(1.5)

    mlp_back(2, NORMED2, ACTIVE2, DOWN2, UP2, UPB, DOWNB, SOUT, DOWN2)

    share_grad(SOUT)
    weight_grad(UP2)
    tick(1.5)
    w_so2 = weight(SO)
    lat_copy.wait_send()

    def mixed_cols(cols):
        dmix[:, cols] = dot_nt(gall[SOUT, 0], w_so2[cols, :]).astype(BF)
    columns_loop(mixed_cols)
    weight_done()

    def attend_back(cols, keep):
        keys = kv[0, :, :, cols].reshape(lat, head_width)
        values = kv[1, :, :, cols].reshape(lat, head_width)
        dm = dmix[:, cols]
        prob_b = pbuf[keep][0]
        prob = prob_b.astype(F32)
        grad = dot_nt(dm, values)
        delta = jnp.sum(prob * grad, axis=1, keepdims=True)
        score = (prob * (grad - delta)).astype(BF)
        gall[SQ, 0, :, cols] = (dot(score, keys) * self_scale).astype(BF)
        dk = (dot_tn(score, qbuf[:, cols]) * self_scale).astype(BF)
        dv = dot_tn(prob_b, dm).astype(BF)
        gall[SK, 0, :, cols] = dk[:count]
        gall[SV, 0, :, cols] = dv[:count]
        kv[0, 1, :, cols] = dk[count:]
        kv[1, 1, :, cols] = dv[count:]
    heads(attend_back)
    unspill = local(pspill, pbuf, 4)
    share_dkv = remote(kv.at[:, 1], dkv_in, peer)
    share_grad(SQ)
    tick(4.0)
    weight_grad(SOUT)
    tick(1.0)
    share_dkv.wait_recv()

    def add_kv(rows):
        for at, m in ((0, SK), (1, SV)):
            gall[m, 0, rows, :] = gall[m, 0, rows, :] + dkv_in[at, rows, :]
    rows_loop(add_kv)
    share_grad(SK)
    share_grad(SV)
    for at, (m, index) in enumerate(((SQ, QW), (SK, KW), (SV, VW))):
        w_now = weight(index)

        def normed_cols(cols, at=at, m=m, w_now=w_now):
            value = dot_nt(gall[m, 0], w_now[cols, :])
            if at == 0:
                dnorm[:, cols] = value
            else:
                dnorm[:, cols] += value
        columns_loop(normed_cols)
        weight_done()
    layer_back(1, SELFN, DOWN1)
    share_grad(DOWN1)
    tick(3.0)
    weight_grad(SQ)
    tick(1.0)
    weight_grad(SK)
    tick(1.0)
    mlp_back(0, NORMED1, ACTIVE1, DOWN1, UP1, UP, DOWN, 0)

    w_o = weight(WO)

    def attended_back(cols):
        gall[1, 0, :, cols] = dot_nt(gall[0, 0], w_o[cols, :]).astype(BF)
    columns_loop(attended_back)
    weight_done()
    share_cd = remote(gall.at[1 - core, 0], gcd_in, peer)
    folded = jnp.concatenate([dot_nt(gall[1, 0], wkv[:MAIN, :]), dot_nt(gall[1, 0], w_rest[...])], axis=1)
    along = jnp.sum(folded * amix[...].astype(F32), axis=0, keepdims=True)
    gsum[3:4, :FEAT_PAD] = along
    gsum[3:4, FEAT_PAD:] = jnp.zeros((1, width - FEAT_PAD), F32)
    da_all[pl.ds(chip, 1), :, pl.ds(core, 1)] = folded.astype(BF).reshape(1, 2, 1, block, FEAT_PAD)
    mine = da_all.at[chip, :, core]
    da_across = remote(mine, mine, across)
    da_peer = remote(mine, mine, peer)
    tick(2.0)
    weight_grad(SV)
    tick(1.0)
    da_across.wait_recv()
    other = da_all.at[1 - chip, :, core]
    da_other = remote(other, other, peer)
    weight_grad(DOWN1)
    tick(1.0)
    weight_grad(UP1)
    tick(1.0)

    share_cd.wait_recv()
    amix_copy.wait_recv()
    lefts = jnp.concatenate([amix[:, :MAIN], amix_in[:, :MAIN]], axis=0)
    grads = jnp.concatenate([gall[pl.ds(core, 1), 0][0], gcd_in[...]], axis=0)
    total = dot_tn(lefts, grads).astype(BF)
    for plane in range(2):
        store_plane(FEATURE_UNIT, plane, total[plane * LANES : (plane + 1) * LANES])
    begin_unit(FEATURE_UNIT)
    for plane in range(2):
        store_plane(INIT_UNIT, plane, upstr[plane * block : (plane + 1) * block, :].astype(BF))
    begin_unit(INIT_UNIT)
    gsum[4:, :] = jnp.zeros((gsum.shape[0] - 4, width), F32)
    rests = [dot_tn(amix[:, MAIN:], gall[side, 0])[:8] for side in range(2)]
    for i in range(8):
        cols = slice(i * LANES, (i + 1) * LANES)
        both = jnp.concatenate([rests[0][:, cols], rests[1][:, cols]], axis=0)
        sm[16 * i : 16 * (i + 1), FEAT_PAD:] = both.astype(BF)
        sm[128 + 16 * i : 128 + 16 * (i + 1), FEAT_PAD:] = gsum[:, cols].astype(BF)
    sm[256:, FEAT_PAD:] = jnp.zeros((lat - 256, LANES), BF)
    tick(2.0)

    da_peer.wait_recv()
    da_other.wait_recv()
    unspill.wait()

    def score_rows(s):
        return wslots.at[s, pl.ds(0, lat)]

    def da_rows(s):
        return wslots.at[s, pl.ds(lat, lat), pl.ds(0, CAT)]

    def q_rows(s):
        return wslots.at[2, pl.ds(s * lat, lat), pl.ds(0, CAT)]

    for s in range(2):
        for i in range(4):
            rows = pl.ds(i * block, block)
            wslots[s, lat + i * block : lat + (i + 1) * block, :CAT] = spread_out(
                da_all[s, i // 2, i % 2], s, rows
            )
            wslots[2, s * lat + i * block : s * lat + (i + 1) * block, :CAT] = spread_out(
                fold[rows, :], s, rows
            )

        def back_cols(cols, s=s):
            fbuf[:, cols] = dot(wslots[s, lat:, :CAT], xcat[s, :, cols])
        columns_loop(back_cols, 256, slots)

        def score_back(rows, s=s):
            prob = pbuf[s, rows, :].astype(F32)
            grad = fbuf[rows, :]
            delta = jnp.sum(prob * grad, axis=1, keepdims=True)
            wslots[s, rows, :] = (prob * (grad - delta)).astype(BF)
        rows_loop(score_back, 64, lat)
        scores = wslots[s, :lat, :]
        zero = dot_nt(scores, xcat[s, :MAIN, :])
        one = dot_nt(scores, xcat[s, MAIN : 2 * MAIN, :])
        rest = dot_nt(scores, xcat[s, 2 * MAIN :, :])
        main, rest = pull_in(s, pl.ds(0, lat), zero, one, rest)
        if s == 0:
            bsum[:, :MAIN] = main
            bsum[:, MAIN:] = rest
        else:
            sm[:, :MAIN] = (bsum[:, :MAIN] + main).astype(BF)
            sm[:, MAIN:FEAT_PAD] = (bsum[:, MAIN:] + rest).astype(BF)
        tick(4.0)

    small_send()
    for copy in act_copies.values():
        copy.wait_send()
    for s in range(2):
        for at, (lo, size) in enumerate(((0, MAIN), (MAIN, MAIN), (2 * MAIN, LANES))):
            cols = pl.ds(lo, size)
            total = dot_tn(wslots[2, s * lat : (s + 1) * lat, cols], wslots[s, :lat, :])
            total = total + dot_tn(wslots[s, lat:, cols], pbuf[s])
            acts[pl.ds(s * CAT + lo, size), :] = total.astype(BF)
            tick(2.0)

    main_gain, rest_gain = gain_col[:MAIN, :], gain_col[MAIN:, :]
    y_copy = None
    for k in range(2):
        if y_copy is not None:
            y_copy.wait()
        for s in range(2):

            def pixel_step(jb, carry, k=k, s=s):
                cols = pl.ds(pl.multiple_of(jb * LANES, LANES), LANES)
                up_main = acts[s * CAT + k * MAIN : s * CAT + (k + 1) * MAIN, cols].astype(F32)
                up_rest = acts[s * CAT + 2 * MAIN : s * CAT + 2 * MAIN + 16, cols].astype(F32)
                up_rest = up_rest[8 * k : 8 * k + 8]
                x_main = xcat[s, k * MAIN : (k + 1) * MAIN, cols].astype(F32)
                x_rest = xcat[s, 2 * MAIN : 2 * MAIN + 16, cols].astype(F32)[8 * k : 8 * k + 8]
                rs = pixel_rs[pl.ds(k * (group // 2) + 2 * jb + s, 1), :]
                scaled_main, scaled_rest = up_main * main_gain, up_rest * rest_gain

                def mean_of(a, b):
                    whole = jnp.sum(a, axis=0, keepdims=True) + jnp.sum(b, axis=0, keepdims=True)
                    return whole * (1.0 / features)
                centre = mean_of(scaled_main, scaled_rest)
                along = mean_of(up_main * x_main, up_rest * x_rest)
                unit_main, unit_rest = x_main / main_gain, x_rest / rest_gain
                out_main = rs * (scaled_main - centre - unit_main * along)
                out_rest = rs * (scaled_rest - centre - unit_rest * along)
                flat[pl.ds(2 * jb + s, tall, stride=group // 2), :] = jnp.concatenate(
                    [out_main, out_rest], axis=0
                )
                return carry
            lax.fori_loop(0, blocks, pixel_step, 0)
            tick(2.0)
        y_copy = local(flat.at[pl.ds(0, features * group // 2)], y_ref.at[k], 7 + k)
    while next_due() < 1e9:
        serve()
    for g, from_chip, own in gathers:
        from_chip.wait_recv()
        span = pl.ds(g[0], len(g))
        remote(fin_in.at[span], gat_ref.at[other_row, span], peer)
        own.wait()
        z_local.append(local(fin_in.at[span], gat_ref.at[other_row, span], 9 + g[0] // 6))
    for copy in z_local + [y_copy]:
        copy.wait()
    for copy in copies:
        copy.finish()


def finish_kernel(*refs):
    it = iter(refs)

    def take(n=None):
        return next(it) if n is None else [next(it) for _ in range(n)]

    y_in, lat_in = take(2)
    ins = take(8)
    query_gain, pixel_gain = take(2)
    y_out, lat_out, init_out, pixel_gain_out, key_out, value_out = take(6)
    gain_outs = take(4)
    mat_outs = take(MATS + 2)
    held = take(8)
    summed, small, fold, init_all, wq, wk, wv, init_sum = held
    unit, normed, total, mats, wk_rest, wv_rest, y_buf, lat_buf, back = take(9)
    sem, out_sem = take(2)
    features, width = ins[5].shape
    lat = init_all.shape[0]
    block = lat // 4
    j = lax.axis_index("seq")
    row = lax.axis_index("row")
    cross_scale = 1.0 / math.sqrt(width)

    through = [
        (pltpu.make_async_copy(y_in.at[k], y_buf.at[:, pl.ds(k * y_in.shape[2], y_in.shape[2])], sem.at[8 + k]))
        for k in range(2)
    ] + [pltpu.make_async_copy(lat_in, lat_buf, sem.at[10])]
    copies = []
    for i, (src, dst) in enumerate(zip(ins, held)):
        copies.append(pltpu.make_async_copy(src, dst, sem.at[i]))
        copies[-1].start()
        if i == 0:
            for copy in through:
                copy.start()
    outs = []

    def put(src, dst):
        copy = pltpu.make_async_copy(src, dst, out_sem.at[len(outs)])
        copy.start()
        outs.append(copy)

    copies[0].wait()
    for m in range(MATS):
        for r in range(4):
            for h in range(2):
                at = (r % 2) * (width // 2) + (r // 2) * 2 * LANES + h * LANES
                mats[m, at : at + LANES, :] = summed[r, 2 * m + h].astype(F32)
        put(mats.at[m], mat_outs[m])
    for copy in through:
        copy.wait()
    put(y_buf, y_out)
    put(lat_buf, lat_out)

    copies[3].wait()
    query_rs = []
    for r in range(4):
        rows = pl.ds(r * block, block)
        value, scale = norm_parts(init_all[rows, :].astype(F32))
        unit[rows, :] = value
        normed[rows, :] = (value * query_gain[...]).astype(BF)
        query_rs.append(scale)
    for copy in copies[1:3] + copies[4:]:
        copy.wait()
    fill_rest(wv_rest, wv)
    fill_rest(wk_rest, wk)
    my_cols = pl.ds(pl.multiple_of(j * LANES, LANES), LANES)

    for n in range(width // 256):
        cols = pl.ds(n * 256, 256)
        value = dot(small[:, :MAIN], wk[:MAIN, cols]) + dot(small[:, MAIN:FEAT_PAD], wk_rest[:, cols])
        total[:, cols] = (value * cross_scale).astype(BF)

    def put_turned(index, value):
        for n in range(width // LANES):
            mats[index, n * LANES : (n + 1) * LANES, :] = value[:, n * LANES : (n + 1) * LANES].T
        put(mats.at[index], mat_outs[index])
    put_turned(MATS, dot_tn(total[:, my_cols], normed[...]))
    outer = [
        [summed[2 * y + c, FEATURE_UNIT].astype(F32) for y in range(2)] for c in range(2)
    ]
    rests = small[pl.ds(pl.multiple_of(j * 16, 16), 16), FEAT_PAD:]
    value_out[:LANES, :] = outer[1][0]
    value_out[LANES:MAIN, :] = outer[1][1]
    value_out[MAIN:, :] = rests.astype(F32)[8 : 8 + features - MAIN]
    summed_c = jnp.concatenate(outer[0], axis=0).astype(BF)
    put_turned(MATS + 1, dot_tn(summed_c, wv[:MAIN, :]) + dot_tn(rests, wv_rest[:16, :]))
    my_queries = dot(normed[...], wq[:, my_cols]).astype(BF)
    key_turned = dot_tn(my_queries, small[:, :FEAT_PAD]) * cross_scale
    key_out[...] = jnp.concatenate(
        [key_turned[:, n * LANES : (n + 1) * LANES].T for n in range(3)], axis=0
    )[:features]
    for i in range(8):
        chunk = small[128 + 16 * i : 128 + 16 * (i + 1), FEAT_PAD:].astype(F32)
        for g in range(3):
            gain_outs[g][i : i + 1, :] = chunk[g : g + 1]
    scores = small[:, :FEAT_PAD].astype(F32)
    part = jnp.sum(fold[...].astype(F32) * scores, axis=0, keepdims=True)
    rest_sum = [small[128 + 16 * i : 128 + 16 * (i + 1), FEAT_PAD:].astype(F32)[3:4] for i in range(3)]
    whole = (part + jnp.concatenate(rest_sum, axis=1))[:, :features]
    pixel_gain_out[...] = (whole / pixel_gain[...].reshape(1, features)).reshape(features)
    own = pl.ds(pl.multiple_of(row * block, block), block)
    own_rs = query_rs[0]
    for r in range(1, 4):
        own_rs = jnp.where(row == r, query_rs[r], own_rs)
    sums = jnp.zeros((block, 1), F32)
    alongs = jnp.zeros((block, 1), F32)
    for n in range(width // 256):
        cols = pl.ds(n * 256, 256)
        back[:, cols] = dot_nt(total[...], wq[cols, :])
        row_sum = jnp.sum(back[:, cols] * unit[:, cols], axis=0, keepdims=True)
        for i in range(2):
            gain_outs[3][2 * n + i : 2 * n + i + 1, :] = row_sum[:, i * LANES : (i + 1) * LANES]
        scaled = back[own, cols] * query_gain[:, cols]
        sums = sums + jnp.sum(scaled, axis=1, keepdims=True)
        alongs = alongs + jnp.sum(scaled * unit[own, cols], axis=1, keepdims=True)
    scaled = back[own, my_cols] * query_gain[:, my_cols]
    query_in = own_rs * (scaled - sums * (1.0 / width) - unit[own, my_cols] * (alongs * (1.0 / width)))
    init_out[...] = init_sum[...].astype(F32) + query_in
    for copy in outs:
        copy.wait()


def finish(y, latents, summed, small, init_sum, fold, init_all, wq, wk, wv, query_gain, pixel_gain):
    features, width = wk.shape
    lat = init_all.shape[0]
    block = lat // 4
    vmem = pl.BlockSpec(memory_space=pltpu.VMEM)
    hbm = pl.BlockSpec(memory_space=pl.ANY)

    def f32(*shape):
        return jax.ShapeDtypeStruct(shape, F32)

    outs = pl.pallas_call(
        finish_kernel,
        out_shape=[f32(features, 2 * y.shape[2], LANES), jax.ShapeDtypeStruct(latents.shape, BF), f32(block, LANES),
                   f32(features), f32(features, LANES), f32(features, LANES)]
        + [f32(width // LANES, LANES)] * 4 + [f32(width, LANES)] * (MATS + 2),
        in_specs=[hbm] * 10 + [vmem] * 2,
        out_specs=[hbm] * 2 + [vmem] * 8 + [hbm] * (MATS + 2),
        scratch_shapes=[
            pltpu.VMEM(shape, BF)
            for shape in (summed.shape, small.shape, fold.shape, init_all.shape,
                          wq.shape, wk.shape, wv.shape, init_sum.shape)
        ]
        + [
            pltpu.VMEM((lat, width), F32),
            pltpu.VMEM((lat, width), BF),
            pltpu.VMEM((lat, width), BF),
            pltpu.VMEM((MATS + 2, width, LANES), F32),
            pltpu.VMEM((LANES, width), BF),
            pltpu.VMEM((LANES, width), BF),
            pltpu.VMEM((features, 2 * y.shape[2], LANES), F32),
            pltpu.VMEM(latents.shape, BF),
            pltpu.VMEM((lat, width), F32),
            pltpu.SemaphoreType.DMA((11,)),
            pltpu.SemaphoreType.DMA((MATS + 4,)),
        ],
        compiler_params=pltpu.CompilerParams(vmem_limit_bytes=VMEM_LIMIT),
    )(y, latents, summed, small, fold, init_all, wq, wk, wv, init_sum, query_gain[None],
      pixel_gain)
    y, latents, init_grad, pixel_gain_grad, key_grad, value_grad = outs[:6]
    return (y, latents, init_grad, outs[6:10], pixel_gain_grad, key_grad, value_grad, outs[10:])


def whole_stack(shards, z, pixel_gain, pseg, init, cots, seg, wk, wv, gains, weights):
    width = init.shape[1]
    block = init.shape[0]
    count = 2 * block
    lat = 2 * count
    share = width // shards
    half = width // 2
    bits = shards.bit_length() - 1
    orders = unit_orders(bits)
    nslots = 3
    features = wk.shape[0]
    group = z.shape[0] // features
    slots = group * LANES // 4
    small, size = [], lat
    for i in range(bits + 2):
        size = size // 2 if size > 16 else size
        small.append((size, 512))
    scratch = [
        ((nslots, width, width), BF),
        (wk.shape, BF),
        ((LANES, width), BF),
        ((2, block, width), BF),
        ((2, 2, block, FEAT_PAD), BF),
        ((2, block, FEAT_PAD), BF),
        ((2, block, FEAT_PAD), BF),
        ((count, FEAT_PAD), BF),
        ((count, FEAT_PAD), BF),
        ((2, 2, 2, block, FEAT_PAD), BF),
        ((lat, width), F32),
        ((3, count, LANES), F32),
        ((6 * count, width), BF),
        ((6, count, half), BF),
        ((2, count, width), BF),
        ((count, width), BF),
        ((2, 2, count, width), BF),
        ((2, lat, slots), BF),
        ((count, width), BF),
        ((2, count, width), BF),
        ((MATS, 2, count, width), BF),
        ((count, width), BF),
        ((FEATURE_UNIT + 1, share, LANES), BF),
        ((2, 2, 2, block, FEAT_PAD), BF),
        ((lat, FEAT_PAD), F32),
        ((16, width), F32),
        ((1, lat), F32),
        ((lat, 512), BF),
        ((2, CAT, slots), BF),
        (((MAIN + 8) * group // 2, LANES), F32),
        ((2, 8, slots), F32),
        ((group, LANES), F32),
        ((MAIN + 8, LANES), F32),
        ((FEATURE_UNIT + 1, share, LANES), BF),
        ((UNITS * 2, width, LANES), BF),
    ]
    for order in orders:
        scratch += [(shape, BF) for shape in stage_shapes(order, width)]
    scratch += [(shape, BF) for shape in small]
    stages = sum(len(order) for order in orders)
    vmem = pl.BlockSpec(memory_space=pltpu.VMEM)
    hbm = pl.BlockSpec(memory_space=pl.ANY)
    return pl.pallas_call(
        functools.partial(
            main_kernel, (shards, width, count, dict(small_stages=len(small)))
        ),
        out_shape=[
            jax.ShapeDtypeStruct((2, block, width), BF),
            jax.ShapeDtypeStruct((lat, 512), BF),
            jax.ShapeDtypeStruct((4, FEATURE_UNIT + 1, share, LANES), BF),
            jax.ShapeDtypeStruct((share, LANES), BF),
            jax.ShapeDtypeStruct((lat, FEAT_PAD), BF),
            jax.ShapeDtypeStruct((4, block, width), BF),
            jax.ShapeDtypeStruct((2, features * group // 2, LANES), F32),
            jax.ShapeDtypeStruct((2, lat, slots), BF),
        ],
        in_specs=[hbm, pl.BlockSpec(memory_space=pltpu.SMEM), vmem, vmem, hbm, vmem]
        + [hbm] * 2 + [vmem] * 4 + [hbm] * 10,
        out_specs=[vmem, vmem, hbm, vmem, vmem, hbm, hbm, hbm],
        scratch_shapes=[pltpu.VMEM(shape, kind) for shape, kind in scratch]
        + [
            pltpu.SemaphoreType.DMA((nslots + 2 + 13,)),
            pltpu.SemaphoreType.DMA((-(-z.shape[0] // width),)),
            pltpu.SemaphoreType.DMA((stages,)),
            pltpu.SemaphoreType.DMA((stages,)),
            pltpu.SemaphoreType.DMA((80,)),
            pltpu.SemaphoreType.DMA((80,)),
        ],
        compiler_params=pltpu.CompilerParams(
            collective_id=0, has_side_effects=True, vmem_limit_bytes=VMEM_LIMIT
        ),
    )(z, pixel_gain, pseg, init, cots, seg, wk, wv, *[g[None] for g in gains], *weights)


VMEM_LIMIT = 63 * 1024 * 1024


def body(
    pixels, pixel_seg, latent_seg, latent_init, cotangent,
    pixel_gain, query_gain, query_weight, key_weight, value_weight, output_weight,
    mlp_gain, up_weight, down_weight,
    self_gain, self_query, self_key, self_value, self_output,
    second_gain, second_up, second_down,
):
    seqs, pix, features = pixels.shape
    block, width = latent_init.shape
    shards = lax.axis_size("seq")
    lat = block * lax.axis_size("row")
    row = lax.axis_index("row")
    cross_scale = 1.0 / math.sqrt(width)
    tiles = pix // LANES

    z = pixels.transpose(2, 0, 1).reshape(features, seqs, tiles, LANES)
    z = z.transpose(0, 2, 1, 3).reshape(features * seqs * tiles, LANES)
    latents, small, summed, init_sum, fold, init_all, y, unused = whole_stack(
        shards, z, pixel_gain, pixel_seg, latent_init, cotangent, latent_seg, key_weight, value_weight,
        (mlp_gain, self_gain, second_gain, query_gain),
        (query_weight, output_weight, up_weight, down_weight, self_query, self_key, self_value,
         self_output, second_up, second_down),
    )
    init_all = init_all.reshape(lat, width)
    y = y.reshape(2, features, tiles, LANES)
    if width // shards == LANES:
        y, latents, init_grad, gains, pixel_gain_grad, key_grad, value_grad, mats = finish(
            y, latents, summed, small, init_sum, fold, init_all, query_weight, key_weight,
            value_weight, query_gain, pixel_gain,
        )
    else:
        y = y.transpose(1, 0, 2, 3)
    pixel_grad = y.reshape(features, tiles, seqs, LANES).transpose(2, 1, 3, 0)
    pixel_grad = pixel_grad.reshape(seqs, pix, features)
    if width // shards == LANES:
        mlp_gain_grad, self_gain_grad, second_gain_grad, query_gain_grad = [
            g.reshape(width) for g in gains
        ]
        return (
            latents, pixel_grad, init_grad, pixel_gain_grad,
            query_gain_grad, mlp_gain_grad, self_gain_grad, second_gain_grad,
            mats[MATS], key_grad, value_grad, mats[MATS + 1], mats[UP1], mats[DOWN1],
            mats[SQ], mats[SK], mats[SV], mats[SOUT], mats[UP2], mats[DOWN2],
        )

    share = width // shards
    at = lax.axis_index("seq") * share

    def columns(arr):
        return lax.dynamic_slice_in_dim(arr, at, share, arr.ndim - 1)

    score_b = small[:, :features]
    side = small[:, FEAT_PAD:]
    rests = side[:128].reshape(8, 2, 8, LANES).transpose(1, 2, 0, 3).reshape(2, 8, width)
    sums = side[128:256].reshape(8, 16, LANES).transpose(1, 0, 2).reshape(16, width).astype(F32)
    pixel_gain_grad = (
        jnp.sum(fold[:, :features].astype(F32) * score_b.astype(F32), axis=0) + sums[3, :features]
    ) / pixel_gain
    units = summed.reshape(2, 2, FEATURE_UNIT + 1, share, LANES)
    mats = units[:, :, :FEATURE_UNIT].reshape(2, 2, MATS, 2, share, LANES)
    mats = mats.transpose(2, 1, 0, 3, 5, 4).reshape(MATS, width, share).astype(F32)
    outer = units[:, :, FEATURE_UNIT].transpose(1, 0, 3, 2).reshape(2, MAIN, share)
    outer = jnp.concatenate([outer, columns(rests)[:, : features - MAIN]], axis=1)
    value_grad = outer[1].astype(F32)
    output_grad = dot_tn(value_weight, outer[0])
    query_unit, query_rs = norm_parts(init_all.astype(F32))
    query_normed = (query_unit * query_gain).astype(BF)
    my_queries = dot(query_normed, columns(query_weight)).astype(BF)
    key_grad = dot_tn(score_b, my_queries) * cross_scale
    query_total = (dot(score_b, key_weight) * cross_scale).astype(BF)
    query_grad = dot_tn(query_normed, columns(query_total))
    query_in, query_gain_grad = norm_back(
        query_unit, query_rs, query_gain, dot_nt(query_total, query_weight)
    )
    init_grad = init_sum.T.astype(F32) + lax.dynamic_slice(query_in, (row * block, at), (block, share))
    return (
        latents, pixel_grad, init_grad,
        pixel_gain_grad, query_gain_grad, sums[0], sums[1], sums[2],
        query_grad, key_grad, value_grad, output_grad, mats[UP1], mats[DOWN1],
        mats[SQ], mats[SK], mats[SV], mats[SOUT], mats[UP2], mats[DOWN2],
    )


def solution(mesh):
    placed = (
        P("seq", "row", None), P("seq", "row"), P("seq", "row"), P("row", None),
        P("seq", "row", None),
    ) + (P(),) * 17
    cols = P(None, "seq")
    return jax.shard_map(
        body,
        mesh=mesh,
        in_specs=placed,
        out_specs=(P("seq", "row", None), P("seq", "row", None), P("row", "seq"))
        + (P(),) * 5 + (cols,) * 12,
        check_vma=False,
    )
```

time: 2450 us -> 174 us (0.07)
  waiting for transfers between devices: 1860 us -> 0 us
  matrix products: 336 us -> 0 us
  Pallas kernels: 0 us -> 173 us
  other arithmetic: 118 us -> 0 us
  blocking collectives: 62.3 us -> 0 us
  local copies, waits for them, and re-layouts: 44.8 us -> 0 us
    reduce_scatter x19 -> x0, waiting for transfers between devices: 1480 us -> none  [the longest x2 319 us: body(): lax.psum_scatter(jnp.concatenate([inner_left(cross_grad, queries) * cross...]
    all_gather x8 -> x0, waiting for transfers between devices: 375 us -> none  [the longest x2 180 us: body(): lax.all_gather(own_values, 'row', axis=0, tiled=True)]
    dot_general x95 -> x0, matrix products: 336 us -> none  [the longest x28 113 us: inner_right(): lax.dot_general(former, latter, (((1,), (1,)), ((), ())), preferred_eleme...]
    pallas_call x0 -> x2, Pallas kernels: none -> 173 us  [the longest x1 160 us: whole_stack(): pl.pallas_call(functools.partial(main_kernel, (shards, width, count, dict...]
    convert_element_type x34 -> x0, other arithmetic: 48.3 us -> none  [the longest x2 12 us: body(): cross_grad = (probs_full * (full_grad - row_sums)).astype(jnp.bfloat16)]
    concatenate x2 -> x0, other arithmetic: 46.2 us -> none  [body(): jnp.concatenate([inner_left(cross_grad, queries) * cross_scale, inner_lef...]
    psum x1 -> x0, blocking collectives: 40.4 us -> none  [body(): lax.psum((gain_sums[0], gain_sums[1], gain_sums[2], gain_sums[3], gain_su...]
    unnamed x373 -> x0, local copies, waits for them, and re-layouts: 30.6 us -> none
  transfers between devices with their start and end apart: 28 -> 0, of which waited for: 27 -> 0; matrix products, arithmetic and copies ran while one was open for 14% -> 0% of each run, Pallas kernels for 0% -> 0%
where the time goes in v1:
time: 174 us
  Pallas kernels  173 us (99%)
    pallas_call x1, Pallas kernels, whole_stack(): pl.pallas_call(functools.partial(main_kernel, (shards, width, count, dict...  160 us
    pallas_call x1, Pallas kernels, finish(): pl.pallas_call(finish_kernel, out_shape=[f32(features, 2 * y.shape[2], LA...  13.3 us

profile of v1, /device:TPU:0, one launch (start us, length us, event | category | flops | bytes accessed | tf_op | source)
XLA Modules:
  0.0 174.1 jit_solution(11192597375857132975)
XLA Ops:
  0.7 159.9 %shard_map.365 = (bf16[2,128,1024]{2,1,0:T(8,128)(2,1)}, bf16[512,512]{1,0:T(8,128)(2,1)}, bf16[4,17,128,128]{3,2,1,0:T(8,128)(2,1)}, bf16[128,128]{1,0:T(8,128)...) custom-call(bf16[8352,128]{1,0:T(8,128)(2,1)} %bitcast.23, ...), custom_call_target="tpu_custom_call" | custom-call | tf_op jit(solution)/shard_map/pallas_call | solution.py:1155
  160.6 13.3 %shard_map.366 = (f32[261,32,128]{2,1,0:T(8,128)}, bf16[2,128,1024]{2,1,0:T(8,128)(2,1)}, f32[128,128]{1,0:T(8,128)}, f32[261]{0:T(512)}, f32[261,128]{1,0:T(8,1...) custom-call(f32[2,261,16,128]{3,2,1,0:T(8,128)} %bitcast.22, ...), custom_call_target="tpu_custom_call" | custom-call | tf_op jit(solution)/shard_map/pallas_call | solution.py:1063

commit v2 on v1

--- a/solution.py
+++ b/solution.py
@@ -96,14 +96,20 @@
         self.wait_send()
 
 
+KINDS = "FCDFBCAEBACCBBAABA"
+
+
 def unit_orders(bits):
-    rest = list(range(bits))
-    head, tail = rest[:2], rest[2:]
-    by_y = ["y"] + rest
-    by_first = head + ["y"] + tail
-    by_second = head[::-1] + ["y"] + tail
-    kinds = [by_y, by_first, by_second]
-    return [kinds[u % 3] for u in range(UNITS)]
+    first, second, tail = [0], list(range(1, min(bits, 2))), list(range(2, bits))
+    kinds = {
+        "A": ["y"] + first + second + tail,
+        "B": first + second + ["y"] + tail,
+        "C": second + first + ["y"] + tail,
+        "D": first + ["y"] + second + tail,
+        "E": second + ["y"] + first + tail,
+        "F": ["y"] + second + first + tail,
+    }
+    return [kinds[letter] for letter in KINDS]
 
 
 def stage_shapes(order, width):
@@ -330,11 +336,12 @@
             s["lo"], s["size"] = pl.multiple_of(keep, share), size
         slot = sum(len(orders[v]) for v in range(u)) + k
         s["copy"] = Remote(copies, src, recv[u][k], usend.at[slot], urecv.at[slot], partner[axis])
-        link = {"y": "y", 0: "x"}.get(axis, "z%s" % axis)
-        begin = max(clock[0], free.get(link, 0.0))
-        took = s["size"] * s["planes"] * LANES * 2 * (2 if link in ("x", "y", "z1") else 4) / 75e3
-        free[link] = begin + took
-        s["due"] = begin + took + 4.0
+        took = s["size"] * s["planes"] * LANES * 2 * 2 / 80e3
+        links = {"y": {"y": 1}, 0: {"x": 1}, 1: {"inner": 1}}.get(axis, {"inner": 1, "middle": 2})
+        begin = max([clock[0]] + [free.get(link, 0.0) for link in links])
+        for link, share_of in links.items():
+            free[link] = begin + took * share_of
+        s["due"] = max(free[link] for link in links) + 4.0
         pending.append(u)
 
     def finish_stage(u):
@@ -743,13 +750,13 @@
         gall[SV, 0, :, cols] = dv[:count]
         kv[0, 1, :, cols] = dk[count:]
         kv[1, 1, :, cols] = dv[count:]
+    weight_grad(SOUT)
+    tick(1.0)
     heads(attend_back)
     unspill = local(pspill, pbuf, 4)
     share_dkv = remote(kv.at[:, 1], dkv_in, peer)
     share_grad(SQ)
     tick(4.0)
-    weight_grad(SOUT)
-    tick(1.0)
     share_dkv.wait_recv()
 
     def add_kv(rows):
@@ -976,11 +983,6 @@
                 at = (r % 2) * (width // 2) + (r // 2) * 2 * LANES + h * LANES
                 mats[m, at : at + LANES, :] = summed[r, 2 * m + h].astype(F32)
         put(mats.at[m], mat_outs[m])
-    for copy in through:
-        copy.wait()
-    put(y_buf, y_out)
-    put(lat_buf, lat_out)
-
     copies[3].wait()
     query_rs = []
     for r in range(4):
@@ -989,6 +991,10 @@
         unit[rows, :] = value
         normed[rows, :] = (value * query_gain[...]).astype(BF)
         query_rs.append(scale)
+    for copy in through:
+        copy.wait()
+    put(y_buf, y_out)
+    put(lat_buf, lat_out)
     for copy in copies[1:3] + copies[4:]:
         copy.wait()
     fill_rest(wv_rest, wv)

time: 174 us -> 172 us (0.989)
  Pallas kernels: 173 us -> 171 us
where the time goes in v2:
time: 172 us
  Pallas kernels  171 us (99%)
    pallas_call x1, Pallas kernels, whole_stack(): pl.pallas_call(functools.partial(main_kernel, (shards, width, count, dict...  160 us
    pallas_call x1, Pallas kernels, finish(): pl.pallas_call(finish_kernel, out_shape=[f32(features, 2 * y.shape[2], LA...  11.6 us

profile of v2, /device:TPU:0, one launch (start us, length us, event | category | flops | bytes accessed | tf_op | source)
XLA Modules:
  0.0 172.0 jit_solution(16367716571586244067)
XLA Ops:
  0.7 159.6 %shard_map.365 = (bf16[2,128,1024]{2,1,0:T(8,128)(2,1)}, bf16[512,512]{1,0:T(8,128)(2,1)}, bf16[4,17,128,128]{3,2,1,0:T(8,128)(2,1)}, bf16[128,128]{1,0:T(8,128)...) custom-call(bf16[8352,128]{1,0:T(8,128)(2,1)} %bitcast.23, ...), custom_call_target="tpu_custom_call" | custom-call | tf_op jit(solution)/shard_map/pallas_call | solution.py:1161
  160.2 11.6 %shard_map.366 = (f32[261,32,128]{2,1,0:T(8,128)}, bf16[2,128,1024]{2,1,0:T(8,128)(2,1)}, f32[128,128]{1,0:T(8,128)}, f32[261]{0:T(512)}, f32[261,128]{1,0:T(8,1...) custom-call(f32[2,261,16,128]{3,2,1,0:T(8,128)} %bitcast.22, ...), custom_call_target="tpu_custom_call" | custom-call | tf_op jit(solution)/shard_map/pallas_call | solution.py:1069

commit v3 on v2

--- a/solution.py
+++ b/solution.py
@@ -67,8 +67,7 @@
 }
 MATS = 8
 FEATURE_UNIT = 2 * MATS
-INIT_UNIT = FEATURE_UNIT + 1
-UNITS = INIT_UNIT + 1
+UNITS = MATS + 1
 
 
 class Remote:
@@ -96,7 +95,7 @@
         self.wait_send()
 
 
-KINDS = "FCDFBCAEBACCBBAABA"
+KINDS = "FCDABCEBA"
 
 
 def unit_orders(bits):
@@ -113,14 +112,13 @@
 
 
 def stage_shapes(order, width):
-    shapes, planes, size = [], 2, width
+    shapes, planes, size = [], 4, width
     for axis in order:
         if axis == "y":
-            planes = 1
-            shapes.append((size, LANES))
+            planes = 2
         else:
             size //= 2
-            shapes.append((2, size, LANES) if planes == 2 else (size, LANES))
+        shapes.append((planes, size, LANES))
     return shapes
 
 
@@ -149,7 +147,7 @@
      sm, xcat, flat, rest0, pixel_rs, gain_col, fin_in, part) = take(35)
     recv = [take(len(orders[u])) for u in range(UNITS)]
     smr = take(sizes["small_stages"])
-    (wsem, zsem, usend, urecv, csend, crecv) = take(6)
+    (wsem, psem, zsem, usend, urecv, csend, crecv) = take(7)
 
     j = lax.axis_index("seq")
     row = lax.axis_index("row")
@@ -172,8 +170,30 @@
     nslots = wslots.shape[0]
     at_use = [0]
 
+    pieces = 4
+
+    class WeightCopy:
+        def __init__(self, i):
+            size = width // pieces
+            self.copies = [
+                pltpu.make_async_copy(
+                    w_hbm[uses[i]].at[pl.ds(p * size, size)],
+                    wslots.at[i % nslots, pl.ds(p * size, size)],
+                    psem.at[(i % nslots) * pieces + p],
+                )
+                for p in range(pieces)
+            ]
+
+        def start(self):
+            for copy in self.copies:
+                copy.start()
+
+        def wait(self):
+            for copy in self.copies:
+                copy.wait()
+
     def weight_copy(i):
-        return pltpu.make_async_copy(w_hbm[uses[i]], wslots.at[i % nslots], wsem.at[i % nslots])
+        return WeightCopy(i)
 
     def weight(expect):
         i = at_use[0]
@@ -317,17 +337,17 @@
     pending = []
 
     def region(u, planes, lo, size):
-        if planes == 2:
-            return part.at[pl.ds(2 * u, 2), pl.ds(lo, size)]
-        return part.at[2 * u + chip, pl.ds(lo, size)]
+        if planes == 4:
+            return part.at[pl.ds(4 * u, 4), pl.ds(lo, size)]
+        return part.at[pl.ds(4 * u + 2 * chip, 2), pl.ds(lo, size)]
 
     def send_stage(u):
         s = state[u]
         axis = orders[u][s["stage"]]
         k = s["stage"]
         if axis == "y":
-            src = part.at[2 * u + 1 - chip, pl.ds(s["lo"], s["size"])]
-            s["planes"] = 1
+            src = part.at[pl.ds(4 * u + 2 - 2 * chip, 2), pl.ds(s["lo"], s["size"])]
+            s["planes"] = 2
         else:
             size = s["size"] // 2
             keep = s["lo"] + bit_of[axis] * size
@@ -349,40 +369,36 @@
         k = s["stage"]
         s["copy"].wait_recv()
         last = k == len(orders[u]) - 1
+        mine = pl.ds(4 * u, 4) if s["planes"] == 4 else pl.ds(4 * u + 2 * chip, 2)
         if last:
-            total = part[pl.ds(2 * u + chip, 1), pl.ds(s["lo"], s["size"])][0] + recv[u][k][...]
-            if u == INIT_UNIT:
-                initg_ref[...] = total
+            total = part[mine, pl.ds(s["lo"], s["size"])] + recv[u][k][...]
+            if u == MATS:
+                fin[FEATURE_UNIT] = total[0]
+                initg_ref[...] = total[1]
             else:
-                fin[u] = total
+                fin[2 * u : 2 * u + 2] = total
             s["done"] = True
             done_units.append(u)
             gather_ready()
             return
         step = min(s["size"], 256)
-        for p in range(s["planes"]):
-            def add(i, carry):
-                off = pl.multiple_of(i * step, step)
-                mine = pl.ds(pl.multiple_of(s["lo"] + off, share), step)
-                if s["planes"] == 2:
-                    got = recv[u][k][p, pl.ds(off, step), :]
-                    part[2 * u + p, mine, :] = part[2 * u + p, mine, :] + got
-                else:
-                    got = recv[u][k][pl.ds(off, step), :]
-                    at = pl.ds(2 * u + chip, 1)
-                    part[at, mine, :] = part[at, mine, :] + got[None]
-                return carry
-            lax.fori_loop(0, s["size"] // step, add, 0)
+
+        def add(i, carry):
+            off = pl.multiple_of(i * step, step)
+            rows = pl.ds(pl.multiple_of(s["lo"] + off, share), step)
+            part[mine, rows, :] = part[mine, rows, :] + recv[u][k][:, pl.ds(off, step), :]
+            return carry
+        lax.fori_loop(0, s["size"] // step, add, 0)
         s["stage"] += 1
         send_stage(u)
 
     done_units, gathers = [], []
-    groups = [list(range(0, 6)), list(range(6, 12)), list(range(12, FEATURE_UNIT + 1))]
+    groups = [[0, 1, 2], [3, 4, 5], [6, 7, 8]]
 
     def gather_ready():
         while len(gathers) < len(groups) and all(u in done_units for u in groups[len(gathers)]):
             g = groups[len(gathers)]
-            span = pl.ds(g[0], len(g))
+            span = pl.ds(2 * g[0], 6 if g[-1] < MATS else 5)
             from_chip = remote(fin.at[span], fin_in.at[span], across)
             remote(fin.at[span], gat_ref.at[row, span], peer)
             gathers.append((g, from_chip, local(fin.at[span], gat_ref.at[row, span], len(gathers))))
@@ -406,7 +422,7 @@
             serve()
 
     def begin_unit(u):
-        state[u] = dict(stage=0, planes=2, lo=0, size=width, done=False)
+        state[u] = dict(stage=0, planes=4, lo=0, size=width, done=False)
         send_stage(u)
 
     def position(u, block):
@@ -416,15 +432,15 @@
             pos = pos + ((block // (1 << b)) % 2) * (1 << (bits - 1 - at))
         return pos
 
-    def store_plane(u, plane, value):
+    def store_plane(u, plane, side, value):
         if share != LANES:
             value = value.astype(F32).T.astype(BF)
         for block_at in range(shards):
             place = pl.ds(position(u, block_at) * share, share)
             if share == LANES:
-                part[pl.ds(2 * u + plane, 1), place, :] = value[:, block_at * share : (block_at + 1) * share][None]
+                part[pl.ds(4 * u + 2 * plane + side, 1), place, :] = value[:, block_at * share : (block_at + 1) * share][None]
             else:
-                part[pl.ds(2 * u + plane, 1), place, :] = value[block_at * share : (block_at + 1) * share][None]
+                part[pl.ds(4 * u + 2 * plane + side, 1), place, :] = value[block_at * share : (block_at + 1) * share][None]
 
     def weight_grad(m):
         left = LEFT[m]
@@ -436,12 +452,11 @@
             theirs = pl.ds(pl.multiple_of(plane * MAIN, MAIN), MAIN)
             lefts = jnp.concatenate([acts[act(left), own], acts_in[left, :, theirs]], axis=0)
             total = dot_tn(lefts, gall[m].reshape(2 * count, width)).astype(BF)
-            store_plane(2 * m, plane, total[:LANES])
-            store_plane(2 * m + 1, plane, total[LANES:])
+            store_plane(m, plane, 0, total[:LANES])
+            store_plane(m, plane, 1, total[LANES:])
             return carry
         lax.fori_loop(0, 2, run, 0)
-        begin_unit(2 * m)
-        begin_unit(2 * m + 1)
+        begin_unit(m)
 
     cot_rows = pl.ds(pl.multiple_of(chip * block, block), block)
     c_own = local(cot_hbm.at[chip], gall.at[DOWN2, 0, cot_rows], 3)
@@ -750,13 +765,13 @@
         gall[SV, 0, :, cols] = dv[:count]
         kv[0, 1, :, cols] = dk[count:]
         kv[1, 1, :, cols] = dv[count:]
-    weight_grad(SOUT)
-    tick(1.0)
     heads(attend_back)
     unspill = local(pspill, pbuf, 4)
     share_dkv = remote(kv.at[:, 1], dkv_in, peer)
     share_grad(SQ)
     tick(4.0)
+    weight_grad(SOUT)
+    tick(1.0)
     share_dkv.wait_recv()
 
     def add_kv(rows):
@@ -817,11 +832,10 @@
     grads = jnp.concatenate([gall[pl.ds(core, 1), 0][0], gcd_in[...]], axis=0)
     total = dot_tn(lefts, grads).astype(BF)
     for plane in range(2):
-        store_plane(FEATURE_UNIT, plane, total[plane * LANES : (plane + 1) * LANES])
-    begin_unit(FEATURE_UNIT)
+        store_plane(MATS, plane, 0, total[plane * LANES : (plane + 1) * LANES])
     for plane in range(2):
-        store_plane(INIT_UNIT, plane, upstr[plane * block : (plane + 1) * block, :].astype(BF))
-    begin_unit(INIT_UNIT)
+        store_plane(MATS, plane, 1, upstr[plane * block : (plane + 1) * block, :].astype(BF))
+    begin_unit(MATS)
     gsum[4:, :] = jnp.zeros((gsum.shape[0] - 4, width), F32)
     rests = [dot_tn(amix[:, MAIN:], gall[side, 0])[:8] for side in range(2)]
     for i in range(8):
@@ -925,10 +939,10 @@
         serve()
     for g, from_chip, own in gathers:
         from_chip.wait_recv()
-        span = pl.ds(g[0], len(g))
+        span = pl.ds(2 * g[0], 6 if g[-1] < MATS else 5)
         remote(fin_in.at[span], gat_ref.at[other_row, span], peer)
         own.wait()
-        z_local.append(local(fin_in.at[span], gat_ref.at[other_row, span], 9 + g[0] // 6))
+        z_local.append(local(fin_in.at[span], gat_ref.at[other_row, span], 9 + g[0] // 3))
     for copy in z_local + [y_copy]:
         copy.wait()
     for copy in copies:
@@ -1150,7 +1164,7 @@
         ((group, LANES), F32),
         ((MAIN + 8, LANES), F32),
         ((FEATURE_UNIT + 1, share, LANES), BF),
-        ((UNITS * 2, width, LANES), BF),
+        ((UNITS * 4, width, LANES), BF),
     ]
     for order in orders:
         scratch += [(shape, BF) for shape in stage_shapes(order, width)]
@@ -1178,6 +1192,7 @@
         scratch_shapes=[pltpu.VMEM(shape, kind) for shape, kind in scratch]
         + [
             pltpu.SemaphoreType.DMA((nslots + 2 + 13,)),
+            pltpu.SemaphoreType.DMA((nslots * 4,)),
             pltpu.SemaphoreType.DMA((-(-z.shape[0] // width),)),
             pltpu.SemaphoreType.DMA((stages,)),
             pltpu.SemaphoreType.DMA((stages,)),

time: 172 us -> 172 us (level)
  no operation moved by 1% of the time
where the time goes in v3:
time: 172 us
  Pallas kernels  171 us (99%)
    pallas_call x1, Pallas kernels, whole_stack(): pl.pallas_call(functools.partial(main_kernel, (shards, width, count, dict...  159 us
    pallas_call x1, Pallas kernels, finish(): pl.pallas_call(finish_kernel, out_shape=[f32(features, 2 * y.shape[2], LA...  11.6 us

profile of v3, /device:TPU:0, one launch (start us, length us, event | category | flops | bytes accessed | tf_op | source)
XLA Modules:
  0.0 171.7 jit_solution(839174231097012729)
XLA Ops:
  0.7 159.2 %shard_map.365 = (bf16[2,128,1024]{2,1,0:T(8,128)(2,1)}, bf16[512,512]{1,0:T(8,128)(2,1)}, bf16[4,17,128,128]{3,2,1,0:T(8,128)(2,1)}, bf16[128,128]{1,0:T(8,128)...) custom-call(bf16[8352,128]{1,0:T(8,128)(2,1)} %bitcast.23, ...), custom_call_target="tpu_custom_call" | custom-call | tf_op jit(solution)/shard_map/pallas_call | solution.py:1175
  159.9 11.6 %shard_map.366 = (f32[261,32,128]{2,1,0:T(8,128)}, bf16[2,128,1024]{2,1,0:T(8,128)(2,1)}, f32[128,128]{1,0:T(8,128)}, f32[261]{0:T(512)}, f32[261,128]{1,0:T(8,1...) custom-call(f32[2,261,16,128]{3,2,1,0:T(8,128)} %bitcast.22, ...), custom_call_target="tpu_custom_call" | custom-call | tf_op jit(solution)/shard_map/pallas_call | solution.py:1083

commit v4 on v3

--- a/solution.py
+++ b/solution.py
@@ -147,7 +147,7 @@
      sm, xcat, flat, rest0, pixel_rs, gain_col, fin_in, part) = take(35)
     recv = [take(len(orders[u])) for u in range(UNITS)]
     smr = take(sizes["small_stages"])
-    (wsem, psem, zsem, usend, urecv, csend, crecv) = take(7)
+    (wsem, psem, zsem, usend, urecv, csend, crecv, hsend, hrecv) = take(9)
 
     j = lax.axis_index("seq")
     row = lax.axis_index("row")
@@ -392,7 +392,7 @@
         s["stage"] += 1
         send_stage(u)
 
-    done_units, gathers = [], []
+    done_units, gathers, forwards = [], [], []
     groups = [[0, 1, 2], [3, 4, 5], [6, 7, 8]]
 
     def gather_ready():
@@ -401,11 +401,22 @@
             span = pl.ds(2 * g[0], 6 if g[-1] < MATS else 5)
             from_chip = remote(fin.at[span], fin_in.at[span], across)
             remote(fin.at[span], gat_ref.at[row, span], peer)
-            gathers.append((g, from_chip, local(fin.at[span], gat_ref.at[row, span], len(gathers))))
+            own = local(fin.at[span], gat_ref.at[row, span], len(gathers))
+            gathers.append((span, from_chip, own))
+            forwards.append((clock[0] + 8.0, len(gathers) - 1))
+
+    def forward(at):
+        span, from_chip, own = gathers[at]
+        from_chip.wait_recv()
+        remote(fin_in.at[span], gat_ref.at[other_row, span], peer)
+        own.wait()
+        z_local.append(local(fin_in.at[span], gat_ref.at[other_row, span], 9 + at))
 
     def serve():
         at = min((state[u]["due"], u) for u in pending) if pending else (1e9, None)
-        if small["due"] <= at[0]:
+        if forwards and forwards[0][0] <= min(at[0], small["due"]):
+            forward(forwards.pop(0)[1])
+        elif small["due"] <= at[0]:
             clock[0] = max(clock[0], small["due"])
             small_step()
         else:
@@ -414,7 +425,7 @@
             finish_stage(at[1])
 
     def next_due():
-        return min([small["due"]] + [state[u]["due"] for u in pending])
+        return min([small["due"]] + [f[0] for f in forwards] + [state[u]["due"] for u in pending])
 
     def tick(us):
         clock[0] += 1.6 * us
@@ -660,7 +671,21 @@
     mlp(0, NORMED1, ACTIVE1, UP, DOWN)
     layer(1, SELFN)
     share_act(SELFN)
-    kv_copies = {}
+    chunks = HEADS // 2
+
+    def chunk_copy(src, dst, at, slot):
+        cols = pl.ds(pl.multiple_of(at * 2 * head_width, 2 * head_width), 2 * head_width)
+        return pltpu.make_async_remote_copy(
+            src_ref=src.at[:, cols], dst_ref=dst.at[:, cols], send_sem=hsend.at[slot + at],
+            recv_sem=hrecv.at[slot + at], device_id=peer, device_id_type=MESH,
+        )
+
+    def kv_chunk(dst, at):
+        return chunk_copy(kv.at[dst, 0], kv.at[dst, 1], at, dst * chunks)
+
+    def dkv_chunk(dst, at):
+        return chunk_copy(kv.at[dst, 1], dkv_in.at[dst], at, (2 + dst) * chunks)
+
     for index, dst in ((KW, 0), (VW, 1), (QW, None)):
         w_now = weight(index)
 
@@ -670,20 +695,19 @@
                 qbuf[:, cols] = value
             else:
                 kv[dst, 0, :, cols] = value
-        columns_loop(project)
+                kv_chunk(dst, cols.start // (2 * head_width)).start()
+        columns_loop(project, 2 * head_width)
         weight_done()
-        if dst is not None:
-            kv_copies[dst] = remote(kv.at[dst, 0], kv.at[dst, 1], peer)
     spill.wait()
-    kv_copies[0].wait_recv()
-    kv_copies[1].wait_recv()
-
-    def heads(body):
+
+    def heads(body, before, after):
         def run(pair, carry):
+            before(pair)
             for side in range(2):
                 cols = pl.ds(pl.multiple_of((2 * pair + side) * head_width, head_width), head_width)
                 rows = pl.ds(pl.multiple_of((pair % 2) * count, count), count)
                 body(cols, (pl.ds(pair // 2, 1), rows, pl.ds(side * lat, lat)))
+            after(pair)
             return carry
         lax.fori_loop(0, HEADS // 2, run, 0)
 
@@ -696,7 +720,12 @@
         prob = (weights * (1.0 / jnp.sum(weights, axis=1, keepdims=True))).astype(BF)
         pbuf[keep] = prob[None]
         acts[act(MIXED), cols] = dot(prob, values).astype(BF)
-    heads(attend)
+
+    def kv_arrived(pair):
+        kv_chunk(0, pair).wait_recv()
+        kv_chunk(1, pair).wait_recv()
+
+    heads(attend, kv_arrived, lambda pair: None)
     share_act(MIXED)
     w_so = weight(SO)
 
@@ -765,14 +794,20 @@
         gall[SV, 0, :, cols] = dv[:count]
         kv[0, 1, :, cols] = dk[count:]
         kv[1, 1, :, cols] = dv[count:]
-    heads(attend_back)
+
+    def dkv_leave(pair):
+        dkv_chunk(0, pair).start()
+        dkv_chunk(1, pair).start()
+
+    heads(attend_back, lambda pair: None, dkv_leave)
     unspill = local(pspill, pbuf, 4)
-    share_dkv = remote(kv.at[:, 1], dkv_in, peer)
     share_grad(SQ)
     tick(4.0)
     weight_grad(SOUT)
     tick(1.0)
-    share_dkv.wait_recv()
+    for at in range(chunks):
+        dkv_chunk(0, at).wait_recv()
+        dkv_chunk(1, at).wait_recv()
 
     def add_kv(rows):
         for at, m in ((0, SK), (1, SV)):
@@ -937,14 +972,12 @@
         y_copy = local(flat.at[pl.ds(0, features * group // 2)], y_ref.at[k], 7 + k)
     while next_due() < 1e9:
         serve()
-    for g, from_chip, own in gathers:
-        from_chip.wait_recv()
-        span = pl.ds(2 * g[0], 6 if g[-1] < MATS else 5)
-        remote(fin_in.at[span], gat_ref.at[other_row, span], peer)
-        own.wait()
-        z_local.append(local(fin_in.at[span], gat_ref.at[other_row, span], 9 + g[0] // 3))
     for copy in z_local + [y_copy]:
         copy.wait()
+    for at in range(chunks):
+        for dst in range(2):
+            kv_chunk(dst, at).wait_send()
+            dkv_chunk(dst, at).wait_send()
     for copy in copies:
         copy.finish()
 
@@ -1198,6 +1231,8 @@
             pltpu.SemaphoreType.DMA((stages,)),
             pltpu.SemaphoreType.DMA((80,)),
             pltpu.SemaphoreType.DMA((80,)),
+            pltpu.SemaphoreType.DMA((16,)),
+            pltpu.SemaphoreType.DMA((16,)),
         ],
         compiler_params=pltpu.CompilerParams(
             collective_id=0, has_side_effects=True, vmem_limit_bytes=VMEM_LIMIT

time: 172 us -> 173 us (level)
  no operation moved by 1% of the time
where the time goes in v4:
time: 173 us; the launch traced here: 172 us
  Pallas kernels  172 us (99%)
    pallas_call x1, Pallas kernels, whole_stack(): pl.pallas_call(functools.partial(main_kernel, (shards, width, count, dict...  160 us
    pallas_call x1, Pallas kernels, finish(): pl.pallas_call(finish_kernel, out_shape=[f32(features, 2 * y.shape[2], LA...  11.6 us

profile of v4, /device:TPU:0, one launch (start us, length us, event | category | flops | bytes accessed | tf_op | source)
XLA Modules:
  0.0 172.4 jit_solution(13950095507474711510)
XLA Ops:
  0.7 160.0 %shard_map.365 = (bf16[2,128,1024]{2,1,0:T(8,128)(2,1)}, bf16[512,512]{1,0:T(8,128)(2,1)}, bf16[4,17,128,128]{3,2,1,0:T(8,128)(2,1)}, bf16[128,128]{1,0:T(8,128)...) custom-call(bf16[8352,128]{1,0:T(8,128)(2,1)} %bitcast.23, ...), custom_call_target="tpu_custom_call" | custom-call | tf_op jit(solution)/shard_map/pallas_call | solution.py:1208
  160.7 11.6 %shard_map.366 = (f32[261,32,128]{2,1,0:T(8,128)}, bf16[2,128,1024]{2,1,0:T(8,128)(2,1)}, f32[128,128]{1,0:T(8,128)}, f32[261]{0:T(512)}, f32[261,128]{1,0:T(8,1...) custom-call(f32[2,261,16,128]{3,2,1,0:T(8,128)} %bitcast.22, ...), custom_call_target="tpu_custom_call" | custom-call | tf_op jit(solution)/shard_map/pallas_call | solution.py:1116

commit v5 on v3

--- a/solution.py
+++ b/solution.py
@@ -144,7 +144,7 @@
     (lat_ref, sm_out, gat_ref, initg_ref, fold, zall, y_ref, pspill) = take(8)
     (wslots, wkv, w_rest, zbuf, ain1, asum, ain2, amix, amix_in, amat, fbuf, rsb, acts, acts_in, slopes,
      qbuf, kv, pbuf, dmix, dkv_in, gall, gcd_in, fin, da_all, bsum, gsum, idrow,
-     sm, xcat, flat, rest0, pixel_rs, gain_col, fin_in, part) = take(35)
+     sm, xcat, flat, rest0, pixel_rs, gain_col, inverse, fin_in, part) = take(36)
     recv = [take(len(orders[u])) for u in range(UNITS)]
     smr = take(sizes["small_stages"])
     (wsem, psem, zsem, usend, urecv, csend, crecv) = take(7)
@@ -246,11 +246,11 @@
             return carry
         lax.fori_loop(0, (total or count) // step, run, 0, unroll=2)
 
-    def columns_loop(body, step=256, total=width):
+    def columns_loop(body, step=512, total=width):
         def run(i, carry):
             body(pl.ds(pl.multiple_of(i * step, step), step))
             return carry
-        lax.fori_loop(0, total // step, run, 0, unroll=2)
+        lax.fori_loop(0, total // step, run, 0)
 
     def layer(k, into):
         def body(rows):
@@ -578,7 +578,7 @@
                 [gall[2 + 2 * turn, 0, :, :CAT], gall[3 + 2 * turn, 0, :, :CAT]], axis=0
             )
             fbuf[:, cols] = dot(queries_cat, xcat[seq, :, cols][0])
-        columns_loop(score_cols, 256, slots)
+        columns_loop(score_cols, 512, slots)
         if turn == 1:
             asum[...] = core_sum(0)
             step2 = remote(asum, ain2, across)
@@ -685,7 +685,7 @@
                 rows = pl.ds(pl.multiple_of((pair % 2) * count, count), count)
                 body(cols, (pl.ds(pair // 2, 1), rows, pl.ds(side * lat, lat)))
             return carry
-        lax.fori_loop(0, HEADS // 2, run, 0)
+        lax.fori_loop(0, HEADS // 2, run, 0, unroll=2)
 
     def attend(cols, keep):
         keys = kv[0, :, :, cols].reshape(lat, head_width)
@@ -871,7 +871,7 @@
 
         def back_cols(cols, s=s):
             fbuf[:, cols] = dot(wslots[s, lat:, :CAT], xcat[s, :, cols])
-        columns_loop(back_cols, 256, slots)
+        columns_loop(back_cols, 512, slots)
 
         def score_back(rows, s=s):
             prob = pbuf[s, rows, :].astype(F32)
@@ -904,6 +904,7 @@
             tick(2.0)
 
     main_gain, rest_gain = gain_col[:MAIN, :], gain_col[MAIN:, :]
+    inverse[...] = 1.0 / gain_col[...]
     y_copy = None
     for k in range(2):
         if y_copy is not None:
@@ -925,7 +926,7 @@
                     return whole * (1.0 / features)
                 centre = mean_of(scaled_main, scaled_rest)
                 along = mean_of(up_main * x_main, up_rest * x_rest)
-                unit_main, unit_rest = x_main / main_gain, x_rest / rest_gain
+                unit_main, unit_rest = x_main * inverse[:MAIN, :], x_rest * inverse[MAIN:, :]
                 out_main = rs * (scaled_main - centre - unit_main * along)
                 out_rest = rs * (scaled_rest - centre - unit_rest * along)
                 flat[pl.ds(2 * jb + s, tall, stride=group // 2), :] = jnp.concatenate(
@@ -1163,6 +1164,7 @@
         ((2, 8, slots), F32),
         ((group, LANES), F32),
         ((MAIN + 8, LANES), F32),
+        ((MAIN + 8, LANES), F32),
         ((FEATURE_UNIT + 1, share, LANES), BF),
         ((UNITS * 4, width, LANES), BF),
     ]

time: 172 us -> 169 us (0.983)
  Pallas kernels: 171 us -> 168 us
    pallas_call x1, Pallas kernels: 159 us -> 157 us  [whole_stack(): pl.pallas_call(functools.partial(main_kernel, (shards, width, count, dict...]
where the time goes in v5:
time: 169 us
  Pallas kernels  168 us (99%)
    pallas_call x1, Pallas kernels, whole_stack(): pl.pallas_call(functools.partial(main_kernel, (shards, width, count, dict...  157 us
    pallas_call x1, Pallas kernels, finish(): pl.pallas_call(finish_kernel, out_shape=[f32(features, 2 * y.shape[2], LA...  11.6 us

profile of v5, /device:TPU:0, one launch (start us, length us, event | category | flops | bytes accessed | tf_op | source)
XLA Modules:
  0.0 169.1 jit_solution(10966040216495886381)
XLA Ops:
  0.7 156.6 %shard_map.365 = (bf16[2,128,1024]{2,1,0:T(8,128)(2,1)}, bf16[512,512]{1,0:T(8,128)(2,1)}, bf16[4,17,128,128]{3,2,1,0:T(8,128)(2,1)}, bf16[128,128]{1,0:T(8,128)...) custom-call(bf16[8352,128]{1,0:T(8,128)(2,1)} %bitcast.23, ...), custom_call_target="tpu_custom_call" | custom-call | tf_op jit(solution)/shard_map/pallas_call | solution.py:1177
  157.3 11.6 %shard_map.366 = (f32[261,32,128]{2,1,0:T(8,128)}, bf16[2,128,1024]{2,1,0:T(8,128)(2,1)}, f32[128,128]{1,0:T(8,128)}, f32[261]{0:T(512)}, f32[261,128]{1,0:T(8,1...) custom-call(f32[2,261,16,128]{3,2,1,0:T(8,128)} %bitcast.22, ...), custom_call_target="tpu_custom_call" | custom-call | tf_op jit(solution)/shard_map/pallas_call | solution.py:1084

commit v6 on v5

--- a/solution.py
+++ b/solution.py
@@ -977,13 +977,11 @@
         (pltpu.make_async_copy(y_in.at[k], y_buf.at[:, pl.ds(k * y_in.shape[2], y_in.shape[2])], sem.at[8 + k]))
         for k in range(2)
     ] + [pltpu.make_async_copy(lat_in, lat_buf, sem.at[10])]
-    copies = []
-    for i, (src, dst) in enumerate(zip(ins, held)):
-        copies.append(pltpu.make_async_copy(src, dst, sem.at[i]))
-        copies[-1].start()
-        if i == 0:
-            for copy in through:
-                copy.start()
+    copies = [
+        pltpu.make_async_copy(src, dst, sem.at[i]) for i, (src, dst) in enumerate(zip(ins, held))
+    ]
+    for copy in [copies[3], copies[0]] + through + [copies[i] for i in (1, 5, 4, 6, 2, 7)]:
+        copy.start()
     outs = []
 
     def put(src, dst):
@@ -991,13 +989,6 @@
         copy.start()
         outs.append(copy)
 
-    copies[0].wait()
-    for m in range(MATS):
-        for r in range(4):
-            for h in range(2):
-                at = (r % 2) * (width // 2) + (r // 2) * 2 * LANES + h * LANES
-                mats[m, at : at + LANES, :] = summed[r, 2 * m + h].astype(F32)
-        put(mats.at[m], mat_outs[m])
     copies[3].wait()
     query_rs = []
     for r in range(4):
@@ -1006,6 +997,13 @@
         unit[rows, :] = value
         normed[rows, :] = (value * query_gain[...]).astype(BF)
         query_rs.append(scale)
+    copies[0].wait()
+    for m in range(MATS):
+        for r in range(4):
+            for h in range(2):
+                at = (r % 2) * (width // 2) + (r // 2) * 2 * LANES + h * LANES
+                mats[m, at : at + LANES, :] = summed[r, 2 * m + h].astype(F32)
+        put(mats.at[m], mat_outs[m])
     for copy in through:
         copy.wait()
     put(y_buf, y_out)

time: 169 us -> 171 us (1.012)
  Pallas kernels: 168 us -> 170 us
    pallas_call x1, Pallas kernels: 11.6 us -> 13.3 us  [finish(): pl.pallas_call(finish_kernel, out_shape=[f32(features, 2 * y.shape[2], LA...]
where the time goes in v6:
time: 171 us
  Pallas kernels  170 us (99%)
    pallas_call x1, Pallas kernels, whole_stack(): pl.pallas_call(functools.partial(main_kernel, (shards, width, count, dict...  157 us
    pallas_call x1, Pallas kernels, finish(): pl.pallas_call(finish_kernel, out_shape=[f32(features, 2 * y.shape[2], LA...  13.3 us

profile of v6, /device:TPU:0, one launch (start us, length us, event | category | flops | bytes accessed | tf_op | source)
XLA Modules:
  0.0 170.8 jit_solution(10959593511866781713)
XLA Ops:
  0.7 156.6 %shard_map.365 = (bf16[2,128,1024]{2,1,0:T(8,128)(2,1)}, bf16[512,512]{1,0:T(8,128)(2,1)}, bf16[4,17,128,128]{3,2,1,0:T(8,128)(2,1)}, bf16[128,128]{1,0:T(8,128)...) custom-call(bf16[8352,128]{1,0:T(8,128)(2,1)} %bitcast.23, ...), custom_call_target="tpu_custom_call" | custom-call | tf_op jit(solution)/shard_map/pallas_call | solution.py:1175
  157.3 13.3 %shard_map.366 = (f32[261,32,128]{2,1,0:T(8,128)}, bf16[2,128,1024]{2,1,0:T(8,128)(2,1)}, f32[128,128]{1,0:T(8,128)}, f32[261]{0:T(512)}, f32[261,128]{1,0:T(8,1...) custom-call(f32[2,261,16,128]{3,2,1,0:T(8,128)} %bitcast.22, ...), custom_call_target="tpu_custom_call" | custom-call | tf_op jit(solution)/shard_map/pallas_call | solution.py:1082
